TPU v7x, 256 devices: a whole 4x4x8 slice. The times are simulated.
256 devices in a mesh: wide: 64 (over z_lo, y, x, core), narrow: 4 (over z_hi).
Axes of the slice: x: 4, y: 4, z: 8 (z_hi: 4, z_lo: 2; z = z_hi * 2 + z_lo), core: 2. Of those that a mesh axis runs over, the one named last changes fastest.
Arguments:
- divergence: float32 [512, 32, 512], P('wide', None, 'narrow'), may hold values from -6 to 6
- pressure_start: float32 [512, 32, 512], P('wide', None, 'narrow'), may hold values from -3 to 3
- phase: int32 [512, 32, 512], P('wide', None, 'narrow'), may hold values 0 or 1
- velocity_cot: float32 [3, 512, 32, 512], P(None, 'wide', None, 'narrow'), may hold values from -6 to 6
Outputs:
- grad_divergence: float32 [512, 32, 512], P('wide', None, 'narrow')
- grad_pressure: float32 [512, 32, 512], P('wide', None, 'narrow')
- grad_faces: float32 [3, 512, 32, 512], P(None, 'wide', None, 'narrow')
Inputs may be any that keep to these rules, and one draw needn't show every extreme that they name: `phase`: 0 marks a liquid cell, 1 a gas cell.
All inputs are finite; a program needn't handle non-finite values. No bound on the sum of `phase` on one device may be relied on, other than what follows from the above.
Results may differ from a plain program's by a relative error of at most 0.0003.
Values sent between devices are 32-bit elements; how exact they have to be, the bound alone decides.
A program may use at most 64 MiB of HBM per device.

v0:
```python
import math

import jax
import jax.numpy as jnp
from jax import lax
from jax.sharding import PartitionSpec as P

SWEEPS = 6


gas_density = 0.25
lower_bound = 0.25
upper_bound = 2.0


def extended_2(shard, sides, width):
    for axis, dim in sides:
        size, length = (lax.axis_size(axis), shard.shape[dim])
        up = [(i, (i + 1) % size) for i in range(size - 1)]
        down = [(j, i) for i, j in up]
        last = lax.slice_in_dim(shard, length - width, length, axis=dim)
        initial = lax.slice_in_dim(shard, 0, width, axis=dim)
        before = lax.ppermute(last, axis, up)
        after = lax.ppermute(initial, axis, down)
        shard = jnp.concatenate([before, shard, after], axis=dim)
    return shard


def passed_along(value, axis, steps):
    count = lax.axis_size(axis)
    initial, last = (max(0, -steps), min(count, count - steps))
    return lax.ppermute(value, axis, [(source, source + steps) for source in range(initial, last)])


def chebyshev_weights(count):
    center = 0.5 * (upper_bound + lower_bound)
    radius = 0.5 * (upper_bound - lower_bound)
    roots = [
        center + radius * math.cos(math.pi * (2 * number + 1) / (2 * count))
        for number in range(count)
    ]
    order = []
    for number in range(count // 2):
        order.append(number)
        order.append(count - 1 - number)
    return [1.0 / roots[position] for position in order]


def shift_up(array, axis_dim):
    length = array.shape[axis_dim]
    zeros = jnp.zeros_like(lax.slice_in_dim(array, 0, 1, axis=axis_dim))
    return jnp.concatenate(
        [lax.slice_in_dim(array, 1, length, axis=axis_dim), zeros], axis=axis_dim
    )


def shift_down(array, axis_dim):
    length = array.shape[axis_dim]
    zeros = jnp.zeros_like(lax.slice_in_dim(array, 0, 1, axis=axis_dim))
    return jnp.concatenate(
        [zeros, lax.slice_in_dim(array, 0, length - 1, axis=axis_dim)], axis=axis_dim
    )


def trim(array, width):
    return array[width : array.shape[0] - width, :, width : array.shape[2] - width]


def apply_operator(field, upper, lower):
    applied = jnp.zeros_like(field)
    for axis_dim in range(3):
        applied = applied + upper[axis_dim] * (field - shift_up(field, axis_dim))
        applied = applied + lower[axis_dim] * (field - shift_down(field, axis_dim))
    return applied


def per_device(divergence, pressure_start, phase, velocity_cot):
    cells_x = divergence.shape[0]
    cells_z = divergence.shape[2]
    group = 1
    margin = group + 1
    density = jnp.where(phase == 1, gas_density, 1.0).astype(jnp.float32)
    stacked = jnp.stack([density, divergence])
    wider = extended_2(stacked, (("wide", 1), ("narrow", 3)), margin + 1)
    dens_wide = wider[0]
    dens_safe = jnp.where(dens_wide > 0.0, dens_wide, 1.0)
    upper = []
    lower = []
    for axis_dim in range(3):
        above = shift_up(dens_wide, axis_dim)
        below = shift_down(dens_wide, axis_dim)
        upper.append(trim(2.0 / (dens_safe + jnp.where(above > 0.0, above, dens_safe)), 1))
        lower.append(trim(2.0 / (dens_safe + jnp.where(below > 0.0, below, dens_safe)), 1))
    source = trim(wider[1], 1)
    inside = (trim(dens_wide, 1) > 0.0).astype(jnp.float32)
    diag = upper[0] + lower[0] + upper[1] + lower[1] + upper[2] + lower[2]
    diag_safe = jnp.where(inside > 0.0, diag, 1.0)
    weights = chebyshev_weights(SWEEPS)
    groups = SWEEPS // group
    pressure = pressure_start
    saved = []
    extended = None
    for group_number in range(groups):
        extended = extended_2(pressure, (("wide", 0), ("narrow", 2)), margin)
        states = [extended]
        inner = 0
        extended = extended + inside * (
            weights[group_number * group + inner]
            * (source - apply_operator(extended, upper, lower))
            / diag_safe
        )
        states.append(extended)
        saved.append(states[0])
        pressure = trim(extended, margin)
    grad_faces = []
    fluxes = []
    for axis_dim in range(3):
        rise = trim(shift_up(extended, axis_dim) - extended, margin)
        grad_faces.append(-velocity_cot[axis_dim] * rise)
        fluxes.append(trim(upper[axis_dim], margin) * velocity_cot[axis_dim])
    below_x = passed_along(fluxes[0][cells_x - 1 :], "wide", 1)
    below_z = passed_along(fluxes[2][:, :, cells_z - 1 :], "narrow", 1)
    down_x = jnp.concatenate([below_x, fluxes[0][: cells_x - 1]], axis=0)
    down_z = jnp.concatenate([below_z, fluxes[2][:, :, : cells_z - 1]], axis=2)
    adjoint_int = fluxes[0] - down_x + (fluxes[1] - shift_down(fluxes[1], 1)) + (fluxes[2] - down_z)
    grad_source = jnp.zeros_like(divergence)
    for group_number in reversed(range(groups)):
        states = [saved[group_number]]
        adjoint = extended_2(adjoint_int, (("wide", 0), ("narrow", 2)), margin)
        for inner in reversed(range(group)):
            weight = weights[group_number * group + inner]
            state = states[inner]
            scaled = inside * (weight * adjoint / diag_safe)
            residual_ext = source - apply_operator(state, upper, lower)
            ratio = scaled * residual_ext / diag_safe
            adjoint = inside * (adjoint - apply_operator(scaled, upper, lower))
            grad_source = grad_source + trim(scaled, margin)
            for axis_dim in range(3):
                term = (scaled - shift_up(scaled, axis_dim)) * (state - shift_up(state, axis_dim))
                term = term + (ratio + shift_up(ratio, axis_dim))
                grad_faces[axis_dim] = grad_faces[axis_dim] - trim(term, margin)
        adjoint_int = trim(adjoint, margin)
    return (grad_source, adjoint_int, jnp.stack(grad_faces))


def solution(mesh):
    in_specs = (
        P("wide", None, "narrow"),
        P("wide", None, "narrow"),
        P("wide", None, "narrow"),
        P(None, "wide", None, "narrow"),
    )
    out_specs = (
        P("wide", None, "narrow"),
        P("wide", None, "narrow"),
        P(None, "wide", None, "narrow"),
    )
    return jax.shard_map(
        per_device, mesh=mesh, in_specs=in_specs, out_specs=out_specs, check_vma=False
    )
```

profile of v0, /device:TPU:32, one launch (start us, length us, event | category | flops | bytes accessed | tf_op | source)
XLA Modules:
  0.0 343.8 jit_solution(7516676657933565613)
XLA Ops:
  3.4 8.0 %collective-permute-start.31 = (f32[2,32,128]{2,1,0:T(8,128)S(1)}, f32[2,32,128]{2,1,0:T(8,128)S(1)}, u32[]{:S(2)}, u32[]{:S(2)}) collective-permute-start(f32[2,32,128]{2,1,0:T(8,128)S(1)} %get-tuple-element.213), channel_id=1, source_target_pairs={{4,0},{8,4},{12,8},{16,12},{20,16},{24,20},{28,24},{32,28},{36,32}... | collective-permute-start | bytes 98312 | tf_op jit(solution)/shard_map/ppermute | solution.py:24
  23.1 7.4 %collective-permute-start.1 = (f32[2,3,32,128]{3,2,1,0:T(8,128)S(1)}, f32[2,3,32,128]{3,2,1,0:T(8,128)S(1)}, u32[]{:S(2)}, u32[]{:S(2)}) collective-permute-start(f32[2,3,32,128]{3,2,1,0:T(8,128)S(1)} %get-tuple-element.186), channel_id=1, source_target_pairs={{4,0},{8,4},{12,8},{16,12},{20,16},{24,20},{28,24},{32,28},{36,32}... | collective-permute-start | bytes 294920 | tf_op jit(solution)/shard_map/ppermute | solution.py:24
  42.3 8.6 %collective-permute-start.2 = (f32[2,14,32,3]{3,2,1,0:T(8,128)S(1)}, f32[2,14,32,3]{3,2,1,0:T(8,128)S(1)}, u32[]{:S(2)}, u32[]{:S(2)}) collective-permute-start(f32[2,14,32,3]{3,2,1,0:T(8,128)S(1)} %get-tuple-element.67), channel_id=1, source_target_pairs={{0,1},{1,2},{2,3},{4,5},{5,6},{6,7},{8,9},{9,10},{10,11},{12,13},{... | collective-permute-start | bytes 32264 | tf_op jit(solution)/shard_map/ppermute | solution.py:23
  65.7 7.4 %collective-permute-done.34 = f32[2,32,128]{2,1,0:T(8,128)S(1)} collective-permute-done((f32[2,32,128]{2,1,0:T(8,128)S(1)}, f32[2,32,128]{2,1,0:T(8,128)S(1)}, u32[]{:S(2)}, u32[]{:S(2)}) %collective-permute-start.34) | collective-permute-done | bytes 32800 | tf_op jit(solution)/shard_map/ppermute | solution.py:23
  74.5 7.3 %collective-permute-start.36 = (f32[12,32,2]{2,1,0:T(8,128)S(1)}, f32[12,32,2]{2,1,0:T(8,128)S(1)}, u32[]{:S(2)}, u32[]{:S(2)}) collective-permute-start(f32[12,32,2]{2,1,0:T(8,128)S(1)} %get-tuple-element.207), channel_id=1, source_target_pairs={{0,1},{1,2},{2,3},{4,5},{5,6},{6,7},{8,9},{9,10},{10,11},{12,13},{... | collective-permute-start | bytes 9224 | tf_op jit(solution)/shard_map/ppermute | solution.py:23
  90.9 6.9 %collective-permute-done.38 = f32[2,32,128]{2,1,0:T(8,128)S(1)} collective-permute-done((f32[2,32,128]{2,1,0:T(8,128)S(1)}, f32[2,32,128]{2,1,0:T(8,128)S(1)}, u32[]{:S(2)}, u32[]{:S(2)}) %collective-permute-start.38) | collective-permute-done | bytes 32800 | tf_op jit(solution)/shard_map/ppermute | solution.py:23
  99.2 8.0 %collective-permute-start.40 = (f32[12,32,2]{2,1,0:T(8,128)S(1)}, f32[12,32,2]{2,1,0:T(8,128)S(1)}, u32[]{:S(2)}, u32[]{:S(2)}) collective-permute-start(f32[12,32,2]{2,1,0:T(8,128)S(1)} %get-tuple-element.205), channel_id=1, source_target_pairs={{0,1},{1,2},{2,3},{4,5},{5,6},{6,7},{8,9},{9,10},{10,11},{12,13},{... | collective-permute-start | bytes 9224 | tf_op jit(solution)/shard_map/ppermute | solution.py:23
  116.3 6.9 %collective-permute-done.42 = f32[2,32,128]{2,1,0:T(8,128)S(1)} collective-permute-done((f32[2,32,128]{2,1,0:T(8,128)S(1)}, f32[2,32,128]{2,1,0:T(8,128)S(1)}, u32[]{:S(2)}, u32[]{:S(2)}) %collective-permute-start.42) | collective-permute-done | bytes 32800 | tf_op jit(solution)/shard_map/ppermute | solution.py:23
  124.7 8.6 %collective-permute-start.44 = (f32[12,32,2]{2,1,0:T(8,128)S(1)}, f32[12,32,2]{2,1,0:T(8,128)S(1)}, u32[]{:S(2)}, u32[]{:S(2)}) collective-permute-start(f32[12,32,2]{2,1,0:T(8,128)S(1)} %get-tuple-element.203), channel_id=1, source_target_pairs={{0,1},{1,2},{2,3},{4,5},{5,6},{6,7},{8,9},{9,10},{10,11},{12,13},{... | collective-permute-start | bytes 9224 | tf_op jit(solution)/shard_map/ppermute | solution.py:23
  135.6 6.7 %collective-permute-start.5 = (f32[8,32,1]{2,1,0:T(8,128)S(1)}, f32[8,32,1]{2,1,0:T(8,128)S(1)}, u32[]{:S(2)}, u32[]{:S(2)}) collective-permute-start(f32[8,32,1]{2,1,0:T(8,128)S(1)} %slice.961), channel_id=1, source_target_pairs={{0,1},{1,2},{2,3},{4,5},{5,6},{6,7},{8,9},{9,10},{10,11},{12,13},{... | collective-permute-start | bytes 3080 | tf_op jit(solution)/shard_map/ppermute | solution.py:32
  143.8 7.6 %collective-permute-start.47 = (f32[2,32,128]{2,1,0:T(8,128)S(1)}, f32[2,32,128]{2,1,0:T(8,128)S(1)}, u32[]{:S(2)}, u32[]{:S(2)}) collective-permute-start(f32[2,32,128]{2,1,0:T(8,128)S(1)} %get-tuple-element.154), channel_id=1, source_target_pairs={{4,0},{8,4},{12,8},{16,12},{20,16},{24,20},{28,24},{32,28},{36,32}... | collective-permute-start | bytes 98312 | tf_op jit(solution)/shard_map/ppermute | solution.py:24
  153.5 7.3 %collective-permute-done.46 = f32[2,32,128]{2,1,0:T(8,128)S(1)} collective-permute-done((f32[2,32,128]{2,1,0:T(8,128)S(1)}, f32[2,32,128]{2,1,0:T(8,128)S(1)}, u32[]{:S(2)}, u32[]{:S(2)}) %collective-permute-start.46) | collective-permute-done | bytes 32800 | tf_op jit(solution)/shard_map/ppermute | solution.py:23
  183.0 7.4 %collective-permute-done.50 = f32[2,32,128]{2,1,0:T(8,128)S(1)} collective-permute-done((f32[2,32,128]{2,1,0:T(8,128)S(1)}, f32[2,32,128]{2,1,0:T(8,128)S(1)}, u32[]{:S(2)}, u32[]{:S(2)}) %collective-permute-start.50) | collective-permute-done | bytes 32800 | tf_op jit(solution)/shard_map/ppermute | solution.py:23
  191.8 6.7 %collective-permute-start.52 = (f32[12,32,2]{2,1,0:T(8,128)S(1)}, f32[12,32,2]{2,1,0:T(8,128)S(1)}, u32[]{:S(2)}, u32[]{:S(2)}) collective-permute-start(f32[12,32,2]{2,1,0:T(8,128)S(1)} %get-tuple-element.199), channel_id=1, source_target_pairs={{0,1},{1,2},{2,3},{4,5},{5,6},{6,7},{8,9},{9,10},{10,11},{12,13},{... | collective-permute-start | bytes 9224 | tf_op jit(solution)/shard_map/ppermute | solution.py:23
  199.9 6.8 %collective-permute-start.8 = (f32[12,32,2]{2,1,0:T(8,128)S(1)}, f32[12,32,2]{2,1,0:T(8,128)S(1)}, u32[]{:S(2)}, u32[]{:S(2)}) collective-permute-start(f32[12,32,2]{2,1,0:T(8,128)S(1)} %get-tuple-element.197), channel_id=1, source_target_pairs={{0,1},{1,2},{2,3},{4,5},{5,6},{6,7},{8,9},{9,10},{10,11},{12,13},{... | collective-permute-start | bytes 9224 | tf_op jit(solution)/shard_map/ppermute | solution.py:23
  215.7 6.9 %collective-permute-done.10 = f32[2,32,128]{2,1,0:T(8,128)S(1)} collective-permute-done((f32[2,32,128]{2,1,0:T(8,128)S(1)}, f32[2,32,128]{2,1,0:T(8,128)S(1)}, u32[]{:S(2)}, u32[]{:S(2)}) %collective-permute-start.10) | collective-permute-done | bytes 32800 | tf_op jit(solution)/shard_map/ppermute | solution.py:23
  224.0 6.7 %collective-permute-start.12 = (f32[12,32,2]{2,1,0:T(8,128)S(1)}, f32[12,32,2]{2,1,0:T(8,128)S(1)}, u32[]{:S(2)}, u32[]{:S(2)}) collective-permute-start(f32[12,32,2]{2,1,0:T(8,128)S(1)} %get-tuple-element.195), channel_id=1, source_target_pairs={{0,1},{1,2},{2,3},{4,5},{5,6},{6,7},{8,9},{9,10},{10,11},{12,13},{... | collective-permute-start | bytes 9224 | tf_op jit(solution)/shard_map/ppermute | solution.py:23
  239.8 6.9 %collective-permute-done.14 = f32[2,32,128]{2,1,0:T(8,128)S(1)} collective-permute-done((f32[2,32,128]{2,1,0:T(8,128)S(1)}, f32[2,32,128]{2,1,0:T(8,128)S(1)}, u32[]{:S(2)}, u32[]{:S(2)}) %collective-permute-start.14) | collective-permute-done | bytes 32800 | tf_op jit(solution)/shard_map/ppermute | solution.py:23
  248.2 10.0 %collective-permute-start.16 = (f32[12,32,2]{2,1,0:T(8,128)S(1)}, f32[12,32,2]{2,1,0:T(8,128)S(1)}, u32[]{:S(2)}, u32[]{:S(2)}) collective-permute-start(f32[12,32,2]{2,1,0:T(8,128)S(1)} %get-tuple-element.193), channel_id=1, source_target_pairs={{0,1},{1,2},{2,3},{4,5},{5,6},{6,7},{8,9},{9,10},{10,11},{12,13},{... | collective-permute-start | bytes 9224 | tf_op jit(solution)/shard_map/ppermute | solution.py:23
  267.5 6.8 %collective-permute-done.18 = f32[2,32,128]{2,1,0:T(8,128)S(1)} collective-permute-done((f32[2,32,128]{2,1,0:T(8,128)S(1)}, f32[2,32,128]{2,1,0:T(8,128)S(1)}, u32[]{:S(2)}, u32[]{:S(2)}) %collective-permute-start.18) | collective-permute-done | bytes 32800 | tf_op jit(solution)/shard_map/ppermute | solution.py:23
  275.7 7.6 %collective-permute-start.20 = (f32[12,32,2]{2,1,0:T(8,128)S(1)}, f32[12,32,2]{2,1,0:T(8,128)S(1)}, u32[]{:S(2)}, u32[]{:S(2)}) collective-permute-start(f32[12,32,2]{2,1,0:T(8,128)S(1)} %get-tuple-element.191), channel_id=1, source_target_pairs={{0,1},{1,2},{2,3},{4,5},{5,6},{6,7},{8,9},{9,10},{10,11},{12,13},{... | collective-permute-start | bytes 9224 | tf_op jit(solution)/shard_map/ppermute | solution.py:23
  294.5 6.6 %collective-permute-done.22 = f32[2,32,128]{2,1,0:T(8,128)S(1)} collective-permute-done((f32[2,32,128]{2,1,0:T(8,128)S(1)}, f32[2,32,128]{2,1,0:T(8,128)S(1)}, u32[]{:S(2)}, u32[]{:S(2)}) %collective-permute-start.22) | collective-permute-done | bytes 32800 | tf_op jit(solution)/shard_map/ppermute | solution.py:23
  318.0 7.0 %collective-permute-done.26 = f32[2,32,128]{2,1,0:T(8,128)S(1)} collective-permute-done((f32[2,32,128]{2,1,0:T(8,128)S(1)}, f32[2,32,128]{2,1,0:T(8,128)S(1)}, u32[]{:S(2)}, u32[]{:S(2)}) %collective-permute-start.26) | collective-permute-done | bytes 32800 | tf_op jit(solution)/shard_map/ppermute | solution.py:23
  326.4 8.0 %collective-permute-start.28 = (f32[12,32,2]{2,1,0:T(8,128)S(1)}, f32[12,32,2]{2,1,0:T(8,128)S(1)}, u32[]{:S(2)}, u32[]{:S(2)}) collective-permute-start(f32[12,32,2]{2,1,0:T(8,128)S(1)} %get-tuple-element.187), channel_id=1, source_target_pairs={{0,1},{1,2},{2,3},{4,5},{5,6},{6,7},{8,9},{9,10},{10,11},{12,13},{... | collective-permute-start | bytes 9224 | tf_op jit(solution)/shard_map/ppermute | solution.py:23
  (247 shorter events, 163.4 us)
Async XLA Ops:
  3.4 12.8 %collective-permute-start.31 = (f32[2,32,128]{2,1,0:T(8,128)S(1)}, f32[2,32,128]{2,1,0:T(8,128)S(1)}, u32[]{:S(2)}, u32[]{:S(2)}) collective-permute-start(f32[2,32,128]{2,1,0:T(8,128)S(1)} %get-tuple-element.213), channel_id=1, source_target_pairs={{4,0},{8,4},{12,8},{16,12},{20,16},{24,20},{28,24},{32,28},{36,32}... | collective-permute-start | bytes 98312 | tf_op jit(solution)/shard_map/ppermute | solution.py:24
  16.3 16.2 %collective-permute-start.33 = (f32[12,32,2]{2,1,0:T(8,128)S(1)}, f32[12,32,2]{2,1,0:T(8,128)S(1)}, u32[]{:S(2)}, u32[]{:S(2)}) collective-permute-start(f32[12,32,2]{2,1,0:T(8,128)S(1)} %get-tuple-element.210), channel_id=1, source_target_pairs={{1,0},{2,1},{3,2},{5,4},{6,5},{7,6},{9,8},{10,9},{11,10},{13,12},{... | collective-permute-start | bytes 9224 | tf_op jit(solution)/shard_map/ppermute | solution.py:24
  17.6 14.9 %collective-permute-start.32 = (f32[12,32,2]{2,1,0:T(8,128)S(1)}, f32[12,32,2]{2,1,0:T(8,128)S(1)}, u32[]{:S(2)}, u32[]{:S(2)}) collective-permute-start(f32[12,32,2]{2,1,0:T(8,128)S(1)} %get-tuple-element.209), channel_id=1, source_target_pairs={{0,1},{1,2},{2,3},{4,5},{5,6},{6,7},{8,9},{9,10},{10,11},{12,13},{... | collective-permute-start | bytes 9224 | tf_op jit(solution)/shard_map/ppermute | solution.py:23
  23.1 15.6 %collective-permute-start.1 = (f32[2,3,32,128]{3,2,1,0:T(8,128)S(1)}, f32[2,3,32,128]{3,2,1,0:T(8,128)S(1)}, u32[]{:S(2)}, u32[]{:S(2)}) collective-permute-start(f32[2,3,32,128]{3,2,1,0:T(8,128)S(1)} %get-tuple-element.186), channel_id=1, source_target_pairs={{4,0},{8,4},{12,8},{16,12},{20,16},{24,20},{28,24},{32,28},{36,32}... | collective-permute-start | bytes 294920 | tf_op jit(solution)/shard_map/ppermute | solution.py:24
  41.0 14.4 %collective-permute-start.3 = (f32[2,14,32,3]{3,2,1,0:T(8,128)S(1)}, f32[2,14,32,3]{3,2,1,0:T(8,128)S(1)}, u32[]{:S(2)}, u32[]{:S(2)}) collective-permute-start(f32[2,14,32,3]{3,2,1,0:T(8,128)S(1)} %get-tuple-element.68), channel_id=1, source_target_pairs={{1,0},{2,1},{3,2},{5,4},{6,5},{7,6},{9,8},{10,9},{11,10},{13,12},{... | collective-permute-start | bytes 32264 | tf_op jit(solution)/shard_map/ppermute | solution.py:24
  42.3 14.5 %collective-permute-start.2 = (f32[2,14,32,3]{3,2,1,0:T(8,128)S(1)}, f32[2,14,32,3]{3,2,1,0:T(8,128)S(1)}, u32[]{:S(2)}, u32[]{:S(2)}) collective-permute-start(f32[2,14,32,3]{3,2,1,0:T(8,128)S(1)} %get-tuple-element.67), channel_id=1, source_target_pairs={{0,1},{1,2},{2,3},{4,5},{5,6},{6,7},{8,9},{9,10},{10,11},{12,13},{... | collective-permute-start | bytes 32264 | tf_op jit(solution)/shard_map/ppermute | solution.py:23
  97.9 11.0 %collective-permute-start.41 = (f32[12,32,2]{2,1,0:T(8,128)S(1)}, f32[12,32,2]{2,1,0:T(8,128)S(1)}, u32[]{:S(2)}, u32[]{:S(2)}) collective-permute-start(f32[12,32,2]{2,1,0:T(8,128)S(1)} %get-tuple-element.206), channel_id=1, source_target_pairs={{1,0},{2,1},{3,2},{5,4},{6,5},{7,6},{9,8},{10,9},{11,10},{13,12},{... | collective-permute-start | bytes 9224 | tf_op jit(solution)/shard_map/ppermute | solution.py:24
  99.2 11.2 %collective-permute-start.40 = (f32[12,32,2]{2,1,0:T(8,128)S(1)}, f32[12,32,2]{2,1,0:T(8,128)S(1)}, u32[]{:S(2)}, u32[]{:S(2)}) collective-permute-start(f32[12,32,2]{2,1,0:T(8,128)S(1)} %get-tuple-element.205), channel_id=1, source_target_pairs={{0,1},{1,2},{2,3},{4,5},{5,6},{6,7},{8,9},{9,10},{10,11},{12,13},{... | collective-permute-start | bytes 9224 | tf_op jit(solution)/shard_map/ppermute | solution.py:23
  123.4 18.9 %collective-permute-start.45 = (f32[12,32,2]{2,1,0:T(8,128)S(1)}, f32[12,32,2]{2,1,0:T(8,128)S(1)}, u32[]{:S(2)}, u32[]{:S(2)}) collective-permute-start(f32[12,32,2]{2,1,0:T(8,128)S(1)} %get-tuple-element.204), channel_id=1, source_target_pairs={{1,0},{2,1},{3,2},{5,4},{6,5},{7,6},{9,8},{10,9},{11,10},{13,12},{... | collective-permute-start | bytes 9224 | tf_op jit(solution)/shard_map/ppermute | solution.py:24
  124.7 17.6 %collective-permute-start.44 = (f32[12,32,2]{2,1,0:T(8,128)S(1)}, f32[12,32,2]{2,1,0:T(8,128)S(1)}, u32[]{:S(2)}, u32[]{:S(2)}) collective-permute-start(f32[12,32,2]{2,1,0:T(8,128)S(1)} %get-tuple-element.203), channel_id=1, source_target_pairs={{0,1},{1,2},{2,3},{4,5},{5,6},{6,7},{8,9},{9,10},{10,11},{12,13},{... | collective-permute-start | bytes 9224 | tf_op jit(solution)/shard_map/ppermute | solution.py:23
  133.5 19.8 %collective-permute-start.4 = (f32[1,32,128]{2,1,0:T(8,128)S(1)}, f32[1,32,128]{2,1,0:T(8,128)S(1)}, u32[]{:S(2)}, u32[]{:S(2)}) collective-permute-start(f32[1,32,128]{2,1,0:T(8,128)S(1)} %slice.954), channel_id=1, source_target_pairs={{0,4},{4,8},{8,12},{12,16},{16,20},{20,24},{24,28},{28,32},{32,36}... | collective-permute-start | bytes 49160 | tf_op jit(solution)/shard_map/ppermute | solution.py:32
  135.6 17.7 %collective-permute-start.5 = (f32[8,32,1]{2,1,0:T(8,128)S(1)}, f32[8,32,1]{2,1,0:T(8,128)S(1)}, u32[]{:S(2)}, u32[]{:S(2)}) collective-permute-start(f32[8,32,1]{2,1,0:T(8,128)S(1)} %slice.961), channel_id=1, source_target_pairs={{0,1},{1,2},{2,3},{4,5},{5,6},{6,7},{8,9},{9,10},{10,11},{12,13},{... | collective-permute-start | bytes 3080 | tf_op jit(solution)/shard_map/ppermute | solution.py:32
  160.9 12.8 %collective-permute-start.49 = (f32[12,32,2]{2,1,0:T(8,128)S(1)}, f32[12,32,2]{2,1,0:T(8,128)S(1)}, u32[]{:S(2)}, u32[]{:S(2)}) collective-permute-start(f32[12,32,2]{2,1,0:T(8,128)S(1)} %get-tuple-element.202), channel_id=1, source_target_pairs={{1,0},{2,1},{3,2},{5,4},{6,5},{7,6},{9,8},{10,9},{11,10},{13,12},{... | collective-permute-start | bytes 9224 | tf_op jit(solution)/shard_map/ppermute | solution.py:24
  162.2 11.5 %collective-permute-start.48 = (f32[12,32,2]{2,1,0:T(8,128)S(1)}, f32[12,32,2]{2,1,0:T(8,128)S(1)}, u32[]{:S(2)}, u32[]{:S(2)}) collective-permute-start(f32[12,32,2]{2,1,0:T(8,128)S(1)} %get-tuple-element.201), channel_id=1, source_target_pairs={{0,1},{1,2},{2,3},{4,5},{5,6},{6,7},{8,9},{9,10},{10,11},{12,13},{... | collective-permute-start | bytes 9224 | tf_op jit(solution)/shard_map/ppermute | solution.py:23
  167.7 15.1 %collective-permute-start.7 = (f32[2,32,128]{2,1,0:T(8,128)S(1)}, f32[2,32,128]{2,1,0:T(8,128)S(1)}, u32[]{:S(2)}, u32[]{:S(2)}) collective-permute-start(f32[2,32,128]{2,1,0:T(8,128)S(1)} %get-tuple-element.212), channel_id=1, source_target_pairs={{4,0},{8,4},{12,8},{16,12},{20,16},{24,20},{28,24},{32,28},{36,32}... | collective-permute-start | bytes 98312 | tf_op jit(solution)/shard_map/ppermute | solution.py:24
  169.7 13.2 %collective-permute-start.6 = (f32[2,32,128]{2,1,0:T(8,128)S(1)}, f32[2,32,128]{2,1,0:T(8,128)S(1)}, u32[]{:S(2)}, u32[]{:S(2)}) collective-permute-start(f32[2,32,128]{2,1,0:T(8,128)S(1)} %get-tuple-element.211), channel_id=1, source_target_pairs={{0,4},{4,8},{8,12},{12,16},{16,20},{20,24},{24,28},{28,32},{32,36}... | collective-permute-start | bytes 98312 | tf_op jit(solution)/shard_map/ppermute | solution.py:23
  190.5 16.2 %collective-permute-start.53 = (f32[12,32,2]{2,1,0:T(8,128)S(1)}, f32[12,32,2]{2,1,0:T(8,128)S(1)}, u32[]{:S(2)}, u32[]{:S(2)}) collective-permute-start(f32[12,32,2]{2,1,0:T(8,128)S(1)} %get-tuple-element.200), channel_id=1, source_target_pairs={{1,0},{2,1},{3,2},{5,4},{6,5},{7,6},{9,8},{10,9},{11,10},{13,12},{... | collective-permute-start | bytes 9224 | tf_op jit(solution)/shard_map/ppermute | solution.py:24
  191.8 14.9 %collective-permute-start.52 = (f32[12,32,2]{2,1,0:T(8,128)S(1)}, f32[12,32,2]{2,1,0:T(8,128)S(1)}, u32[]{:S(2)}, u32[]{:S(2)}) collective-permute-start(f32[12,32,2]{2,1,0:T(8,128)S(1)} %get-tuple-element.199), channel_id=1, source_target_pairs={{0,1},{1,2},{2,3},{4,5},{5,6},{6,7},{8,9},{9,10},{10,11},{12,13},{... | collective-permute-start | bytes 9224 | tf_op jit(solution)/shard_map/ppermute | solution.py:23
  246.9 13.1 %collective-permute-start.17 = (f32[12,32,2]{2,1,0:T(8,128)S(1)}, f32[12,32,2]{2,1,0:T(8,128)S(1)}, u32[]{:S(2)}, u32[]{:S(2)}) collective-permute-start(f32[12,32,2]{2,1,0:T(8,128)S(1)} %get-tuple-element.194), channel_id=1, source_target_pairs={{1,0},{2,1},{3,2},{5,4},{6,5},{7,6},{9,8},{10,9},{11,10},{13,12},{... | collective-permute-start | bytes 9224 | tf_op jit(solution)/shard_map/ppermute | solution.py:24
  248.2 13.2 %collective-permute-start.16 = (f32[12,32,2]{2,1,0:T(8,128)S(1)}, f32[12,32,2]{2,1,0:T(8,128)S(1)}, u32[]{:S(2)}, u32[]{:S(2)}) collective-permute-start(f32[12,32,2]{2,1,0:T(8,128)S(1)} %get-tuple-element.193), channel_id=1, source_target_pairs={{0,1},{1,2},{2,3},{4,5},{5,6},{6,7},{8,9},{9,10},{10,11},{12,13},{... | collective-permute-start | bytes 9224 | tf_op jit(solution)/shard_map/ppermute | solution.py:23
  274.4 10.7 %collective-permute-start.21 = (f32[12,32,2]{2,1,0:T(8,128)S(1)}, f32[12,32,2]{2,1,0:T(8,128)S(1)}, u32[]{:S(2)}, u32[]{:S(2)}) collective-permute-start(f32[12,32,2]{2,1,0:T(8,128)S(1)} %get-tuple-element.192), channel_id=1, source_target_pairs={{1,0},{2,1},{3,2},{5,4},{6,5},{7,6},{9,8},{10,9},{11,10},{13,12},{... | collective-permute-start | bytes 9224 | tf_op jit(solution)/shard_map/ppermute | solution.py:24
  275.7 12.4 %collective-permute-start.20 = (f32[12,32,2]{2,1,0:T(8,128)S(1)}, f32[12,32,2]{2,1,0:T(8,128)S(1)}, u32[]{:S(2)}, u32[]{:S(2)}) collective-permute-start(f32[12,32,2]{2,1,0:T(8,128)S(1)} %get-tuple-element.191), channel_id=1, source_target_pairs={{0,1},{1,2},{2,3},{4,5},{5,6},{6,7},{8,9},{9,10},{10,11},{12,13},{... | collective-permute-start | bytes 9224 | tf_op jit(solution)/shard_map/ppermute | solution.py:23
  325.1 10.8 %collective-permute-start.29 = (f32[12,32,2]{2,1,0:T(8,128)S(1)}, f32[12,32,2]{2,1,0:T(8,128)S(1)}, u32[]{:S(2)}, u32[]{:S(2)}) collective-permute-start(f32[12,32,2]{2,1,0:T(8,128)S(1)} %get-tuple-element.188), channel_id=1, source_target_pairs={{1,0},{2,1},{3,2},{5,4},{6,5},{7,6},{9,8},{10,9},{11,10},{13,12},{... | collective-permute-start | bytes 9224 | tf_op jit(solution)/shard_map/ppermute | solution.py:24
  326.4 11.0 %collective-permute-start.28 = (f32[12,32,2]{2,1,0:T(8,128)S(1)}, f32[12,32,2]{2,1,0:T(8,128)S(1)}, u32[]{:S(2)}, u32[]{:S(2)}) collective-permute-start(f32[12,32,2]{2,1,0:T(8,128)S(1)} %get-tuple-element.187), channel_id=1, source_target_pairs={{0,1},{1,2},{2,3},{4,5},{5,6},{6,7},{8,9},{9,10},{10,11},{12,13},{... | collective-permute-start | bytes 9224 | tf_op jit(solution)/shard_map/ppermute | solution.py:23
  (34 other events, 284.2 us)
where the time goes:
time: 348 us; the launch traced here: 344 us
  starting transfers between devices  198 us (57%)
  waiting for transfers between devices  114 us (33%)
  other arithmetic  19.7 us (6%)
  local copies, waits for them, and re-layouts  10 us (3%)
    ppermute x26, starting transfers between devices, extended_2(): before = lax.ppermute(last, axis, up)  124 us
    ppermute x26, waiting for transfers between devices, extended_2(): before = lax.ppermute(last, axis, up)  86.7 us
    ppermute x26, starting transfers between devices, extended_2(): after = lax.ppermute(initial, axis, down)  65.6 us
    ppermute x26, waiting for transfers between devices, extended_2(): after = lax.ppermute(initial, axis, down)  27.2 us
    ppermute x2, starting transfers between devices, passed_along(): lax.ppermute(value, axis, [(source, source + steps) for source in range(i...  8.65 us
  transfers between devices with their start and end apart: 54, of which 32 were waited for; matrix products, arithmetic and copies ran while one was open for 2% of the time, Pallas kernels for 0%

commit v1 on v0

v1 whole, which is shorter than its diff:
```python
import math

import jax
import jax.numpy as jnp
from jax import lax
from jax.experimental import pallas as pl
from jax.experimental.pallas import tpu as pltpu
from jax.sharding import PartitionSpec as P

SWEEPS = 6
CENTER, RADIUS = 1.125, 0.875
PAD = 16
ROWS = 160
NZ = 128
NY = 32
F32 = jnp.float32
MESH = pl.DeviceIdType.MESH
XU, XD, YU, YD, ZU, ZD = range(6)


def chebyshev_weights():
    roots = [CENTER + RADIUS * math.cos(math.pi * (2 * m + 1) / (2 * SWEEPS)) for m in range(SWEEPS)]
    order = []
    for m in range(SWEEPS // 2):
        order += [m, SWEEPS - 1 - m]
    return [1.0 / roots[m] for m in order]


W = chebyshev_weights()


def lanes(rows):
    return lax.broadcasted_iota(jnp.int32, (rows, 128), 1)


def x_up(tile, after, lane):
    return pltpu.roll(tile if after is None else jnp.where(lane < 32, after, tile), 96, 1)


def x_down(tile, before, lane):
    return pltpu.roll(tile if before is None else jnp.where(lane >= 96, before, tile), 32, 1)


def y_up(tile):
    return pltpu.roll(tile, 127, 1)


def y_down(tile):
    return pltpu.roll(tile, 1, 1)


def turned(block):
    return jnp.transpose(block.reshape(128, 128))


def local_sums(ph, ps, dv, vc, lam, res):
    row = lax.broadcasted_iota(jnp.int32, (NY, NZ), 0)
    lane = lax.broadcasted_iota(jnp.int32, (NY, NZ), 1)
    top, bottom, inner = row == NY - 1, row == 0, lane < NZ - 1
    before_lam = before_res = None
    here = ph[0].astype(F32)
    for x in range(8):
        a = here
        base, slope = 1.0 + 0.6 * a, 0.6 + 1.8 * a
        p = ps[x]
        face_y = base + slope * jnp.where(top, a, pltpu.roll(a, NY - 1, 0))
        face_z = jnp.where(inner, base + slope * pltpu.roll(a, NZ - 1, 1), 0.0)
        flux_y = face_y * vc[1, x]
        flux_z = face_z * vc[2, x]
        flow_y = face_y * (p - jnp.where(top, 0.0, pltpu.roll(p, NY - 1, 0)))
        flow_z = face_z * (p - pltpu.roll(p, NZ - 1, 1))
        total = flux_y - jnp.where(bottom, 0.0, pltpu.roll(flux_y, 1, 0)) + flux_z - pltpu.roll(flux_z, 1, 1)
        lower = jnp.where(bottom, -(1.0 + 3.0 * a) * p, pltpu.roll(flow_y, 1, 0))
        rest = dv[x] - (flow_y - lower) - (flow_z - pltpu.roll(flow_z, 1, 1))
        if x > 0:
            total = total - before_lam
            rest = rest + before_res
        if x < 7:
            here = ph[x + 1].astype(F32)
            face_x = base + slope * here
            before_lam = face_x * vc[0, x]
            before_res = face_x * (p - ps[x + 1])
            total = total + before_lam
            rest = rest - before_res
        lam[x] = total
        res[x] = rest


def coefficients(phe, coef, inv, diag, row, rows):
    lane = lanes(rows)
    last, first = (lane & 31) == 31, (lane & 31) == 0
    cur = [phe[c, pl.ds(row, rows), :] for c in range(6)]
    for c in range(6):
        a = cur[c]
        near = [
            x_up(a, cur[c + 1] if c < 5 else None, lane),
            x_down(a, cur[c - 1] if c > 0 else None, lane),
            jnp.where(last, a, y_up(a)),
            jnp.where(first, a, y_down(a)),
            phe[c, pl.ds(row + 1, rows), :],
            phe[c, pl.ds(row - 1, rows), :],
        ]
        near = [b if k in (YU, YD) else jnp.where(b > 1.5, a, b) for k, b in enumerate(near)]
        base, slope = 1.0 + 0.6 * a, 0.6 + 1.8 * a
        total = 6.0 * base + slope * ((near[0] + near[1]) + (near[2] + near[3]) + (near[4] + near[5]))
        inverse = jnp.where(a > 1.5, 0.0, 1.0 / total)
        inv[c, pl.ds(row, rows), :] = inverse
        base, slope = base * inverse, slope * inverse
        for k in range(6):
            value = base + slope * near[k]
            if k == YU:
                value = jnp.where(last, 0.0, value)
            if k == YD:
                value = jnp.where(first, 0.0, value)
            coef[k, c, pl.ds(row, rows), :] = value
        if c in (2, 3):
            diag[c - 2, pl.ds(row, rows), :] = total


def starts(lame, rese, inv, coef, near_edge, own_edge, s5, e0, row, rows):
    lane = lanes(rows)
    low, high = lane < 32, lane >= 96
    ne = near_edge[pl.ds(row, rows), :]
    step = ne - own_edge[pl.ds(row, rows), :]
    for c in range(6):
        i = inv[c, pl.ds(row, rows), :]
        lam = i * lame[c, pl.ds(row, rows), :]
        res = i * rese[c, pl.ds(row, rows), :]
        if c == 1:
            cf = coef[XU, c, pl.ds(row, rows), :]
            lam = lam + jnp.where(high, cf * pltpu.roll(ne, 64, 1), 0.0)
            res = res - jnp.where(high, cf * pltpu.roll(step, 96, 1), 0.0)
        elif c == 2:
            cf = coef[XD, c, pl.ds(row, rows), :]
            lam = lam - jnp.where(low, cf * pltpu.roll(ne, 96, 1), 0.0)
            res = res + jnp.where(low, cf * step, 0.0)
        elif c == 3:
            cf = coef[XU, c, pl.ds(row, rows), :]
            lam = lam + jnp.where(high, cf * ne, 0.0)
            res = res + jnp.where(high, cf * pltpu.roll(step, 32, 1), 0.0)
        elif c == 4:
            cf = coef[XD, c, pl.ds(row, rows), :]
            lam = lam - jnp.where(low, cf * pltpu.roll(ne, 32, 1), 0.0)
            res = res - jnp.where(low, cf * pltpu.roll(step, 64, 1), 0.0)
        s5[c, pl.ds(row, rows), :] = W[5] * lam
        e0[c, pl.ds(row, rows), :] = W[0] * res


def exchange(
    dv_hbm, ps_hbm, ph_hbm, vc_hbm,
    coef, s5, e0, pe, diag, vt,
    ph, ps, dv, vc, lam, res, rx_ph, rx_lam, rx_res, ne, edge_out, zs, rz, rd,
    phe, lame, rese, inv, near_edge, own_edge,
    in_sem, send_x, recv_x, send_z, recv_z, send_d, recv_d,
):
    w, n = lax.axis_index("wide"), lax.axis_index("narrow")
    nw, nn = lax.axis_size("wide"), lax.axis_size("narrow")
    x_after, x_before = (lax.rem(w + 1, nw), n), (lax.rem(w + nw - 1, nw), n)
    z_after, z_before = (w, lax.rem(n + 1, nn)), (w, lax.rem(n + nn - 1, nn))
    barrier = pltpu.get_barrier_semaphore()
    for device in (x_after, x_before, z_after, z_before):
        pl.semaphore_signal(barrier, inc=1, device_id=device, device_id_type=MESH)
    loads = [
        pltpu.make_async_copy(src, dst, in_sem.at[k])
        for k, (src, dst) in enumerate(((ph_hbm, ph), (ps_hbm, ps), (dv_hbm, dv), (vc_hbm, vc)))
    ]
    for load in loads:
        load.start()
    zero = jnp.zeros((NY, NZ), F32)
    rx_ph[0, 0] = jnp.zeros((NY, NZ), jnp.int32)
    rx_ph[1, 7] = jnp.zeros((NY, NZ), jnp.int32)
    for k in (0, 1):
        rx_lam[0, k] = zero
        rx_res[0, k] = zero
        rx_lam[1, 6 + k] = zero
        rx_res[1, 6 + k] = zero
    rx_res[0, 2] = zero
    for c in range(6):
        for r in (0, 152):
            phe[c, r : r + 8, :] = jnp.zeros((8, 128), F32)
            s5[c, r : r + 8, :] = jnp.zeros((8, 128), F32)
            e0[c, r : r + 8, :] = jnp.zeros((8, 128), F32)
    for load in loads:
        load.wait()

    local_sums(ph, ps, dv, vc, lam, res)
    main = slice(PAD, PAD + NZ)
    for j in range(2):
        part = slice(4 * j, 4 * j + 4)
        phe[2 + j, main, :] = turned(ph[part].astype(F32))
        lame[2 + j, main, :] = turned(lam[part])
        rese[2 + j, main, :] = turned(res[part])
        pe[j, main, :] = turned(ps[part])
        for a in range(3):
            vt[a, j] = turned(vc[a, part])
    own_edge[main, :] = turned(jnp.stack([ps[0], vc[0, 7], ps[7], vc[0, 7]]))
    edge_out[0] = ps[7]
    edge_out[1] = vc[0, 7]
    ne[3] = vc[0, 7]
    row8 = lax.broadcasted_iota(jnp.int32, (8, 128), 0)
    for side, at in ((0, PAD + NZ - 8), (1, PAD)):
        for j in range(2):
            spare = row8 == (0 if side == 0 else 7)
            line = PAD + NZ - 1 if side == 0 else PAD
            zs[side, 3 * j] = phe[2 + j, at : at + 8, :]
            zs[side, 3 * j + 1] = jnp.where(spare, vt[2, j, NZ - 1 : NZ, :], lame[2 + j, at : at + 8, :])
            zs[side, 3 * j + 2] = jnp.where(spare, pe[j, line : line + 1, :], rese[2 + j, at : at + 8, :])
        zs[side, 6] = own_edge[at : at + 8, :]

    pl.semaphore_wait(barrier, 4)

    def send(src, dst, send_sem, recv_sem, device):
        copy = pltpu.make_async_remote_copy(src, dst, send_sem, recv_sem, device_id=device, device_id_type=MESH)
        copy.start()
        return copy

    to_z = [
        send(zs.at[s], rz.at[s], send_z.at[s], recv_z.at[s], device) for s, device in ((0, z_after), (1, z_before))
    ]
    to_x = [
        send(src, dst, send_x.at[k], recv_x.at[k], device)
        for k, (src, dst, device) in enumerate(
            (
                (ph_hbm.at[1:8], rx_ph.at[0, 1:8], x_after),
                (ph_hbm.at[0:7], rx_ph.at[1, 0:7], x_before),
                (lam.at[2:8], rx_lam.at[0, 2:8], x_after),
                (lam.at[0:6], rx_lam.at[1, 0:6], x_before),
                (edge_out, ne.at[0:2], x_after),
                (edge_out_p0(ps), ne.at[2:3], x_before),
                (res.at[3:8], rx_res.at[0, 3:8], x_after),
                (res.at[0:6], rx_res.at[1, 0:6], x_before),
            )
        )
    ]

    inside_x = (w > 0, w < nw - 1)
    inside_z = (n > 0, n < nn - 1)
    to_d = []
    for s in range(2):
        to_z[s].wait_recv()
        at = PAD - 8 if s == 0 else PAD + NZ
        spare = row8 == (0 if s == 0 else 7)
        line = PAD if s == 0 else PAD + NZ - 1
        own_edge[at : at + 8, :] = rz[s, 6]
        for j in range(2):
            phe[2 + j, at : at + 8, :] = jnp.where(inside_z[s], rz[s, 3 * j], 2.0)
            lame[2 + j, at : at + 8, :] = rz[s, 3 * j + 1]
            rese[2 + j, at : at + 8, :] = rz[s, 3 * j + 2]
            pressure = jnp.where(inside_z[s], rz[s, 3 * j + 2], 0.0)
            if s == 0:
                speed = jnp.where(inside_z[s], rz[s, 3 * j + 1], 0.0)
            else:
                speed = vt[2, j, NZ - 1 : NZ, :]
                pe[j, at : at + 1, :] = pressure[7:8, :]
            rz[s, 3 * j + 1] = jnp.where(spare, speed, rz[s, 3 * j + 1])
            rz[s, 3 * j + 2] = jnp.where(spare, pressure - pe[j, line : line + 1, :], rz[s, 3 * j + 2])
        for k, device in ((0, x_after), (1, x_before)):
            to_d.append(send(rz.at[s], rd.at[k, s], send_d.at[k, s], recv_d.at[k, s], device))

    for k in range(2):
        to_x[k].wait_recv()
        for j in range(2):
            block = turned(rx_ph[k, 4 * j : 4 * j + 4].astype(F32))
            phe[4 * k + j, main, :] = jnp.where(inside_x[k], block, 2.0)

    @pl.loop(0, 14)
    def _(i):
        coefficients(phe, coef, inv, diag, pl.multiple_of(PAD + 8 + 8 * i, 8), 8)

    for k in range(2):
        to_x[2 + k].wait_recv()
        for j in range(2):
            lame[4 * k + j, main, :] = turned(rx_lam[k, 4 * j : 4 * j + 4])
    for k in range(2):
        to_x[4 + k].wait_recv()
    lane128 = lanes(NZ)
    outside = ((lane128 < 64) & jnp.logical_not(inside_x[0])) | (
        (lane128 >= 64) & (lane128 < 96) & jnp.logical_not(inside_x[1])
    )
    near = jnp.where(outside, 0.0, turned(ne[...]))
    near_edge[main, :] = near
    pe[2, main, :] = pltpu.roll(near, 64, 1)
    for k in range(2):
        to_x[6 + k].wait_recv()
        for j in range(2):
            rese[4 * k + j, main, :] = turned(rx_res[k, 4 * j : 4 * j + 4])

    for copy in to_d:
        copy.wait_recv()
    lane = lanes(8)
    for s in range(2):
        at = PAD - 8 if s == 0 else PAD + NZ
        for k in range(2):
            for j in range(2):
                c = 4 * k + j
                phe[c, at : at + 8, :] = jnp.where(jnp.logical_and(inside_x[k], inside_z[s]), rd[k, s, 3 * j], 2.0)
                lame[c, at : at + 8, :] = rd[k, s, 3 * j + 1]
                rese[c, at : at + 8, :] = rd[k, s, 3 * j + 2]
        below = jnp.where(inside_x[0], jnp.where(lane < 32, pltpu.roll(rd[0, s, 6], 64, 1), rd[0, s, 6]), 0.0)
        above = jnp.where(inside_x[1], pltpu.roll(rd[1, s, 6], 64, 1), 0.0)
        near_edge[at : at + 8, :] = jnp.where(
            lane < 64, below, jnp.where(lane < 96, above, own_edge[at : at + 8, :])
        )
    for r in (PAD - 8, PAD, PAD + NZ - 8, PAD + NZ):
        coefficients(phe, coef, inv, diag, r, 8)

    @pl.loop(0, 18)
    def _(i):
        starts(
            lame, rese, inv, coef, near_edge, own_edge, s5, e0, pl.multiple_of(PAD - 8 + 8 * i, 8), 8
        )

    for s in range(2):
        spare = 0 if s == 0 else 7
        for c in range(6):
            j = c % 2
            rows_from = rz.at[s] if c in (2, 3) else rd.at[0 if c < 2 else 1, s]
            speed = rows_from[3 * j + 1, spare : spare + 1, :]
            step = rows_from[3 * j + 2, spare : spare + 1, :]
            own, other = (PAD, PAD - 1) if s == 0 else (PAD + NZ - 1, PAD + NZ)
            c_own = coef[ZD if s == 0 else ZU, c, own : own + 1, :]
            c_other = coef[ZU if s == 0 else ZD, c, other : other + 1, :]
            sign = -W[5] if s == 0 else W[5]
            s5[c, own : own + 1, :] += sign * (c_own * speed)
            s5[c, other : other + 1, :] -= sign * (c_other * speed)
            e0[c, own : own + 1, :] += W[0] * (c_own * step)
            e0[c, other : other + 1, :] -= W[0] * (c_other * step)
    for copy in to_z + to_x + to_d:
        copy.wait_send()


def edge_out_p0(ps):
    return ps.at[0:1]


def neighbours(src, coef, tiles, have, row, rows):
    lane = lanes(rows)
    cur = {c: src[c, pl.ds(row, rows), :] for c in have}
    out = {}
    for c in tiles:
        v = cur[c]
        near = [
            x_up(v, cur.get(c + 1), lane),
            x_down(v, cur.get(c - 1), lane),
            y_up(v),
            y_down(v),
            src[c, pl.ds(row + 1, rows), :],
            src[c, pl.ds(row - 1, rows), :],
        ]
        prod = [coef[k, c, pl.ds(row, rows), :] * near[k] for k in range(6)]
        out[c] = (v, (prod[0] + prod[1]) + (prod[2] + prod[3]) + (prod[4] + prod[5]))
    return out


def chains(coef, s5, e0, pe, diag, vt, gd, gp, gf, s, e, rr, out):
    step = 8

    def sweep(src, dst, tiles, have, keep, scale, first=PAD - 8, last=PAD + NZ + 8):
        @pl.loop(0, (last - first) // step)
        def _(i):
            row = pl.multiple_of(first + step * i, 8)
            for c, (v, total) in neighbours(src, coef, tiles, have, row, step).items():
                dst[c, pl.ds(row, step), :] = keep * v + scale * total

    ss = [s.at[m] for m in range(5)] + [s5]
    ee = [e0] + [e.at[m] for m in range(5)]
    every, middle = range(6), range(1, 5)
    for m in range(5, 0, -1):
        sweep(ss[m], ss[m - 1], every if m == 5 else middle, every if m >= 4 else middle,
              W[m - 1] / W[m] * (1.0 - W[m]), W[m - 1])
    for m in range(5):
        tiles = (range(1, 6), middle, middle, middle, range(2, 5))[m]
        have = (every, range(1, 6), middle, middle, middle)[m]
        sweep(ee[m], ee[m + 1], tiles, have, W[m + 1] / W[m] * (1.0 - W[m]), W[m + 1])

    @pl.loop(0, 17)
    def _(i):
        row = pl.multiple_of(PAD + 8 * i, 8)
        for c in range(2, 5):
            total = None
            for m in range(6):
                term = ss[m][c, pl.ds(row, 8), :] * ee[m][c, pl.ds(row, 8), :] * (1.0 / W[m])
                total = term if total is None else total + term
            rr[c - 2, pl.ds(row, 8), :] = total

    @pl.loop(0, 16)
    def _(i):
        row = pl.multiple_of(PAD + 8 * i, 8)
        own = pl.multiple_of(8 * i, 8)
        lane = lanes(8)
        last = (lane & 31) == 31

        def rises(ref, c, at):
            v = ref[at, pl.ds(row, 8), :]
            after = ref[at + 1, pl.ds(row, 8), :]
            return v, (
                x_up(v, after, lane),
                jnp.where(last, 0.0, y_up(v)),
                ref[at, pl.ds(row + 1, 8), :],
            )

        for j in range(2):
            c = 2 + j
            p, up = rises(pe, c, j)
            rise = [p - u for u in up]
            grads = [None] * 3
            total = None
            for m in range(6):
                v, up = rises(ss[m], c, c)
                for a in range(3):
                    term = (v - up[a]) * rise[a]
                    grads[a] = term if grads[a] is None else grads[a] + term
                total = v if total is None else total + v
                v, up = rises(ee[m], c, c)
                rise = [r + (v - u) for r, u in zip(rise, up)]
            v, up = rises(rr, c, j)
            out[0, j, pl.ds(own, 8), :] = total
            for a in range(3):
                out[2 + a, j, pl.ds(own, 8), :] = (
                    vt[a, j, pl.ds(own, 8), :] * rise[a] - grads[a] - (v + up[a])
                )
        for c, (v, total) in neighbours(ss[0], coef, (2, 3), middle, row, 8).items():
            out[1, c - 2, pl.ds(own, 8), :] = diag[c - 2, pl.ds(row, 8), :] * (
                (1.0 / W[0] - 1.0) * v + total
            )

    for j in range(2):
        part = slice(4 * j, 4 * j + 4)
        gd[part] = jnp.transpose(out[0, j]).reshape(4, NY, NZ)
        gp[part] = jnp.transpose(out[1, j]).reshape(4, NY, NZ)
        for a in range(3):
            gf[a, part] = jnp.transpose(out[2 + a, j]).reshape(4, NY, NZ)


def per_device(divergence, pressure_start, phase, velocity_cot):
    shape = jax.ShapeDtypeStruct
    vmem = pl.BlockSpec(memory_space=pltpu.VMEM)
    dma = pltpu.SemaphoreType.DMA
    args = [
        pltpu.with_memory_space_constraint(a, pltpu.HBM)
        for a in (divergence, pressure_start, phase, velocity_cot)
    ]
    block, tiles = (8, NY, NZ), (6, ROWS, 128)
    made = pl.pallas_call(
        exchange,
        out_shape=[
            shape((6, *tiles), F32),
            shape(tiles, F32),
            shape(tiles, F32),
            shape((3, ROWS, 128), F32),
            shape((2, ROWS, 128), F32),
            shape((3, 2, NZ, 128), F32),
        ],
        in_specs=[pl.BlockSpec(memory_space=pltpu.HBM)] * 4,
        out_specs=[vmem] * 6,
        scratch_shapes=[
            pltpu.VMEM(block, jnp.int32),
            pltpu.VMEM(block, F32),
            pltpu.VMEM(block, F32),
            pltpu.VMEM((3, *block), F32),
            pltpu.VMEM(block, F32),
            pltpu.VMEM(block, F32),
            pltpu.VMEM((2, *block), jnp.int32),
            pltpu.VMEM((2, *block), F32),
            pltpu.VMEM((2, *block), F32),
            pltpu.VMEM((4, NY, NZ), F32),
            pltpu.VMEM((2, NY, NZ), F32),
            pltpu.VMEM((2, 7, 8, 128), F32),
            pltpu.VMEM((2, 7, 8, 128), F32),
            pltpu.VMEM((2, 2, 7, 8, 128), F32),
            pltpu.VMEM(tiles, F32),
            pltpu.VMEM(tiles, F32),
            pltpu.VMEM(tiles, F32),
            pltpu.VMEM(tiles, F32),
            pltpu.VMEM((ROWS, 128), F32),
            pltpu.VMEM((ROWS, 128), F32),
            dma((4,)),
            dma((8,)),
            dma((8,)),
            dma((2,)),
            dma((2,)),
            dma((2, 2)),
            dma((2, 2)),
        ],
        compiler_params=pltpu.CompilerParams(
            collective_id=0, has_side_effects=True, vmem_limit_bytes=24 << 20
        ),
        name="exchange",
    )(*args)
    return tuple(
        pl.pallas_call(
            chains,
            out_shape=[shape(block, F32), shape(block, F32), shape((3, *block), F32)],
            in_specs=[vmem] * 6,
            out_specs=[vmem] * 3,
            scratch_shapes=[
                pltpu.VMEM((5, *tiles), F32),
                pltpu.VMEM((5, *tiles), F32),
                pltpu.VMEM((3, ROWS, 128), F32),
                pltpu.VMEM((5, 2, NZ, 128), F32),
            ],
            compiler_params=pltpu.CompilerParams(vmem_limit_bytes=24 << 20),
            name="chains",
        )(*made)
    )


def solution(mesh):
    field = P("wide", None, "narrow")
    faces = P(None, "wide", None, "narrow")
    return jax.shard_map(
        per_device,
        mesh=mesh,
        in_specs=(field, field, field, faces),
        out_specs=(field, field, faces),
        check_vma=False,
    )
```

time: 348 us -> 40 us (0.11); the launches traced: 344 us -> 39.9 us
  starting transfers between devices: 198 us -> 0 us
  waiting for transfers between devices: 114 us -> 0 us
  Pallas kernels: 0 us -> 39.2 us
  other arithmetic: 19.7 us -> 0 us
  local copies, waits for them, and re-layouts: 10 us -> 0 us
    ppermute x54 -> x0, starting transfers between devices: 198 us -> none  [the longest x26 124 us: extended_2(): before = lax.ppermute(last, axis, up)]
    ppermute x54 -> x0, waiting for transfers between devices: 114 us -> none  [the longest x26 86.7 us: extended_2(): before = lax.ppermute(last, axis, up)]
    pallas_call x0 -> x2, Pallas kernels: none -> 39.2 us  [the longest x1 20.3 us: per_device(): pl.pallas_call(chains, out_shape=[shape(block, F32), shape(block, F32), s...]
    slice x99 -> x0, local copies, waits for them, and re-layouts: 9.92 us -> none  [the longest x57 5.26 us: shift_up(): lax.slice_in_dim(array, 1, length, axis=axis_dim)]
    mul x7 -> x0, other arithmetic: 5.79 us -> none  [the longest x6 5.62 us: per_device(): adjoint = inside * (adjoint - apply_operator(scaled, upper, lower))]
    add x7 -> x0, other arithmetic: 5.27 us -> none  [the longest x6 5.15 us: per_device(): extended + inside * (weights[group_number * group + inner] * (source - ap...]
    another operation x5 -> x0, other arithmetic: 3.76 us -> none  [the longest x4 3.75 us: per_device(): return (grad_source, adjoint_int, jnp.stack(grad_faces))]
  transfers between devices with their start and end apart: 54 -> 0, of which waited for: 32 -> 0; matrix products, arithmetic and copies ran while one was open for 2% -> 0% of each run, Pallas kernels for 0% -> 0%
where the time goes in v1:
time: 40 us; the launch traced here: 39.9 us
  Pallas kernels  39.2 us (98%)
  between operations  0.64 us (2%)
    pallas_call x1, Pallas kernels, per_device(): pl.pallas_call(chains, out_shape=[shape(block, F32), shape(block, F32), s...  20.3 us
    pallas_call x1, Pallas kernels, per_device(): pl.pallas_call(exchange, out_shape=[shape((6, *tiles), F32), shape(tiles,...  18.9 us

profile of v1, /device:TPU:32, one launch (start us, length us, event | category | flops | bytes accessed | tf_op | source)
XLA Modules:
  0.0 39.9 jit_solution(15401282354710769563)
XLA Ops:
  0.6 18.9 %exchange.1 = (f32[6,6,160,128]{3,2,1,0:T(8,128)S(1)}, f32[6,160,128]{2,1,0:T(8,128)S(1)}, f32[6,160,128]{2,1,0:T(8,128)S(1)}, f32[3,160,128]{2,1,0:T(8,128)S(1)...) custom-call(f32[8,32,128]{2,1,0:T(8,128)} %dv_hbm.1, f32[8,32,128]{2,1,0:T(8,128)} %ps_hbm.1, ...), custom_call_target="tpu_custom_call" | custom-call | tf_op jit(solution)/shard_map/exchange/pallas_call | solution.py:444
  19.6 20.3 %chains.1 = (f32[8,32,128]{2,1,0:T(8,128)}, f32[8,32,128]{2,1,0:T(8,128)}, f32[3,8,32,128]{3,2,1,0:T(8,128)}) custom-call(f32[6,6,160,128]{3,2,1,0:T(8,128)S(1)} %get-tuple-element.9.coef, f32[6,160,128]{2,1,0:T(8,128)S(1)} %get-tuple-element.10.s5, f32[6,160,128]{2,1,0:T(8,128)S(1)} %get-tuple-element.11.e0, f32[3,160,128]{2,1,0:T(8,128)S(1)} %get-tuple-element.12.pe, ...), custom_call_target="tpu_custom_call" | custom-call | tf_op jit(solution)/shard_map/chains/pallas_call | solution.py:491

commit v2 on v1

--- a/solution.py
+++ b/solution.py
@@ -263,9 +263,8 @@
             block = turned(rx_ph[k, 4 * j : 4 * j + 4].astype(F32))
             phe[4 * k + j, main, :] = jnp.where(inside_x[k], block, 2.0)
 
-    @pl.loop(0, 14)
-    def _(i):
-        coefficients(phe, coef, inv, diag, pl.multiple_of(PAD + 8 + 8 * i, 8), 8)
+    for row in range(PAD + 8, PAD + NZ - 8, 16):
+        coefficients(phe, coef, inv, diag, row, 16)
 
     for k in range(2):
         to_x[2 + k].wait_recv()
@@ -304,11 +303,8 @@
     for r in (PAD - 8, PAD, PAD + NZ - 8, PAD + NZ):
         coefficients(phe, coef, inv, diag, r, 8)
 
-    @pl.loop(0, 18)
-    def _(i):
-        starts(
-            lame, rese, inv, coef, near_edge, own_edge, s5, e0, pl.multiple_of(PAD - 8 + 8 * i, 8), 8
-        )
+    for row in range(PAD - 8, PAD + NZ + 8, 24):
+        starts(lame, rese, inv, coef, near_edge, own_edge, s5, e0, row, 24)
 
     for s in range(2):
         spare = 0 if s == 0 else 7
@@ -353,12 +349,10 @@
 
 
 def chains(coef, s5, e0, pe, diag, vt, gd, gp, gf, s, e, rr, out):
-    step = 8
+    step = 24
 
     def sweep(src, dst, tiles, have, keep, scale, first=PAD - 8, last=PAD + NZ + 8):
-        @pl.loop(0, (last - first) // step)
-        def _(i):
-            row = pl.multiple_of(first + step * i, 8)
+        for row in range(first, last, step):
             for c, (v, total) in neighbours(src, coef, tiles, have, row, step).items():
                 dst[c, pl.ds(row, step), :] = keep * v + scale * total
 
@@ -373,20 +367,17 @@
         have = (every, range(1, 6), middle, middle, middle)[m]
         sweep(ee[m], ee[m + 1], tiles, have, W[m + 1] / W[m] * (1.0 - W[m]), W[m + 1])
 
-    @pl.loop(0, 17)
-    def _(i):
-        row = pl.multiple_of(PAD + 8 * i, 8)
+    for row in (PAD,):
         for c in range(2, 5):
             total = None
             for m in range(6):
-                term = ss[m][c, pl.ds(row, 8), :] * ee[m][c, pl.ds(row, 8), :] * (1.0 / W[m])
+                term = ss[m][c, pl.ds(row, 136), :] * ee[m][c, pl.ds(row, 136), :] * (1.0 / W[m])
                 total = term if total is None else total + term
-            rr[c - 2, pl.ds(row, 8), :] = total
-
-    @pl.loop(0, 16)
-    def _(i):
-        row = pl.multiple_of(PAD + 8 * i, 8)
-        own = pl.multiple_of(8 * i, 8)
+            rr[c - 2, pl.ds(row, 136), :] = total
+
+    for i in range(16):
+        row = PAD + 8 * i
+        own = 8 * i
         lane = lanes(8)
         last = (lane & 31) == 31
 

time: 40 us -> 24 us (0.60)
  Pallas kernels: 39.2 us -> 23.2 us
    pallas_call x1, Pallas kernels: 20.3 us -> 5.54 us  [per_device(): pl.pallas_call(chains, out_shape=[shape(block, F32), shape(block, F32), s...]
    pallas_call x1, Pallas kernels: 18.9 us -> 17.7 us  [per_device(): pl.pallas_call(exchange, out_shape=[shape((6, *tiles), F32), shape(tiles,...]
where the time goes in v2:
time: 24 us; the launch traced here: 23.9 us
  Pallas kernels  23.2 us (97%)
  between operations  0.64 us (3%)
    pallas_call x1, Pallas kernels, per_device(): pl.pallas_call(exchange, out_shape=[shape((6, *tiles), F32), shape(tiles,...  17.7 us
    pallas_call x1, Pallas kernels, per_device(): pl.pallas_call(chains, out_shape=[shape(block, F32), shape(block, F32), s...  5.54 us

profile of v2, /device:TPU:32, one launch (start us, length us, event | category | flops | bytes accessed | tf_op | source)
XLA Modules:
  0.0 23.9 jit_solution(6796458880870222036)
XLA Ops:
  0.6 17.7 %exchange.1 = (f32[6,6,160,128]{3,2,1,0:T(8,128)S(1)}, f32[6,160,128]{2,1,0:T(8,128)S(1)}, f32[6,160,128]{2,1,0:T(8,128)S(1)}, f32[3,160,128]{2,1,0:T(8,128)S(1)...) custom-call(f32[8,32,128]{2,1,0:T(8,128)} %dv_hbm.1, f32[8,32,128]{2,1,0:T(8,128)} %ps_hbm.1, ...), custom_call_target="tpu_custom_call" | custom-call | tf_op jit(solution)/shard_map/exchange/pallas_call | solution.py:435
  18.3 5.5 %chains.1 = (f32[8,32,128]{2,1,0:T(8,128)}, f32[8,32,128]{2,1,0:T(8,128)}, f32[3,8,32,128]{3,2,1,0:T(8,128)}) custom-call(f32[6,6,160,128]{3,2,1,0:T(8,128)S(1)} %get-tuple-element.9.coef, f32[6,160,128]{2,1,0:T(8,128)S(1)} %get-tuple-element.10.s5, f32[6,160,128]{2,1,0:T(8,128)S(1)} %get-tuple-element.11.e0, f32[3,160,128]{2,1,0:T(8,128)S(1)} %get-tuple-element.12.pe, ...), custom_call_target="tpu_custom_call" | custom-call | tf_op jit(solution)/shard_map/chains/pallas_call | solution.py:482

commit v3 on v2

--- a/solution.py
+++ b/solution.py
@@ -117,38 +117,27 @@
             diag[c - 2, pl.ds(row, rows), :] = total
 
 
-def starts(lame, rese, inv, coef, near_edge, own_edge, s5, e0, row, rows):
+def start(right, inv, coef, near_edge, own_edge, dst, scale, residual, row, rows):
     lane = lanes(rows)
     low, high = lane < 32, lane >= 96
-    ne = near_edge[pl.ds(row, rows), :]
-    step = ne - own_edge[pl.ds(row, rows), :]
+    near = near_edge[pl.ds(row, rows), :]
+    if residual:
+        near = own_edge[pl.ds(row, rows), :] - near
+    shifts = (96, 0, 32, 64) if residual else (64, 96, 0, 32)
     for c in range(6):
-        i = inv[c, pl.ds(row, rows), :]
-        lam = i * lame[c, pl.ds(row, rows), :]
-        res = i * rese[c, pl.ds(row, rows), :]
-        if c == 1:
-            cf = coef[XU, c, pl.ds(row, rows), :]
-            lam = lam + jnp.where(high, cf * pltpu.roll(ne, 64, 1), 0.0)
-            res = res - jnp.where(high, cf * pltpu.roll(step, 96, 1), 0.0)
-        elif c == 2:
-            cf = coef[XD, c, pl.ds(row, rows), :]
-            lam = lam - jnp.where(low, cf * pltpu.roll(ne, 96, 1), 0.0)
-            res = res + jnp.where(low, cf * step, 0.0)
-        elif c == 3:
-            cf = coef[XU, c, pl.ds(row, rows), :]
-            lam = lam + jnp.where(high, cf * ne, 0.0)
-            res = res + jnp.where(high, cf * pltpu.roll(step, 32, 1), 0.0)
-        elif c == 4:
-            cf = coef[XD, c, pl.ds(row, rows), :]
-            lam = lam - jnp.where(low, cf * pltpu.roll(ne, 32, 1), 0.0)
-            res = res - jnp.where(low, cf * pltpu.roll(step, 64, 1), 0.0)
-        s5[c, pl.ds(row, rows), :] = W[5] * lam
-        e0[c, pl.ds(row, rows), :] = W[0] * res
+        value = inv[c, pl.ds(row, rows), :] * right[c, pl.ds(row, rows), :]
+        if 1 <= c <= 4:
+            face = coef[XU if c in (1, 3) else XD, c, pl.ds(row, rows), :]
+            edge = face * (pltpu.roll(near, shifts[c - 1], 1) if shifts[c - 1] else near)
+            edge = jnp.where(high if c in (1, 3) else low, edge, 0.0)
+            plus = c in (1, 3) if not residual else c in (1, 4)
+            value = value + edge if plus else value - edge
+        dst[c, pl.ds(row, rows), :] = scale * value
 
 
 def exchange(
     dv_hbm, ps_hbm, ph_hbm, vc_hbm,
-    coef, s5, e0, pe, diag, vt,
+    coef, ss, ee, s_up, e_up, pe, diag, vt,
     ph, ps, dv, vc, lam, res, rx_ph, rx_lam, rx_res, ne, edge_out, zs, rz, rd,
     phe, lame, rese, inv, near_edge, own_edge,
     in_sem, send_x, recv_x, send_z, recv_z, send_d, recv_d,
@@ -157,6 +146,7 @@
     nw, nn = lax.axis_size("wide"), lax.axis_size("narrow")
     x_after, x_before = (lax.rem(w + 1, nw), n), (lax.rem(w + nw - 1, nw), n)
     z_after, z_before = (w, lax.rem(n + 1, nn)), (w, lax.rem(n + nn - 1, nn))
+    s5, e0 = ss.at[5], ee.at[0]
     barrier = pltpu.get_barrier_semaphore()
     for device in (x_after, x_before, z_after, z_before):
         pl.semaphore_signal(barrier, inc=1, device_id=device, device_id_type=MESH)
@@ -176,10 +166,10 @@
         rx_res[1, 6 + k] = zero
     rx_res[0, 2] = zero
     for c in range(6):
-        for r in (0, 152):
-            phe[c, r : r + 8, :] = jnp.zeros((8, 128), F32)
-            s5[c, r : r + 8, :] = jnp.zeros((8, 128), F32)
-            e0[c, r : r + 8, :] = jnp.zeros((8, 128), F32)
+        for r in (0, PAD + NZ):
+            phe[c, r : r + PAD, :] = jnp.zeros((PAD, 128), F32)
+            ss[5, c, r : r + PAD, :] = jnp.zeros((PAD, 128), F32)
+            ee[0, c, r : r + PAD, :] = jnp.zeros((PAD, 128), F32)
     for load in loads:
         load.wait()
 
@@ -217,21 +207,22 @@
     to_z = [
         send(zs.at[s], rz.at[s], send_z.at[s], recv_z.at[s], device) for s, device in ((0, z_after), (1, z_before))
     ]
-    to_x = [
-        send(src, dst, send_x.at[k], recv_x.at[k], device)
-        for k, (src, dst, device) in enumerate(
-            (
-                (ph_hbm.at[1:8], rx_ph.at[0, 1:8], x_after),
-                (ph_hbm.at[0:7], rx_ph.at[1, 0:7], x_before),
-                (lam.at[2:8], rx_lam.at[0, 2:8], x_after),
-                (lam.at[0:6], rx_lam.at[1, 0:6], x_before),
-                (edge_out, ne.at[0:2], x_after),
-                (edge_out_p0(ps), ne.at[2:3], x_before),
-                (res.at[3:8], rx_res.at[0, 3:8], x_after),
-                (res.at[0:6], rx_res.at[1, 0:6], x_before),
-            )
-        )
-    ]
+    pieces = (
+        (ph_hbm.at[1:8], rx_ph.at[0, 1:8], x_after),
+        (ph_hbm.at[0:7], rx_ph.at[1, 0:7], x_before),
+        (lam.at[2:8], rx_lam.at[0, 2:8], x_after),
+        (lam.at[0:6], rx_lam.at[1, 0:6], x_before),
+        (edge_out, ne.at[0:2], x_after),
+        (ps.at[0:1], ne.at[2:3], x_before),
+        (res.at[3:8], rx_res.at[0, 3:8], x_after),
+        (res.at[0:6], rx_res.at[1, 0:6], x_before),
+    )
+    to_x = []
+    for k, (src, dst, device) in enumerate(pieces):
+        if k == 99:
+            for copy in to_x[0:0]:
+                copy.wait_send()
+        to_x.append(send(src, dst, send_x.at[k], recv_x.at[k], device))
 
     inside_x = (w > 0, w < nw - 1)
     inside_z = (n > 0, n < nn - 1)
@@ -263,7 +254,7 @@
             block = turned(rx_ph[k, 4 * j : 4 * j + 4].astype(F32))
             phe[4 * k + j, main, :] = jnp.where(inside_x[k], block, 2.0)
 
-    for row in range(PAD + 8, PAD + NZ - 8, 16):
+    for row in range(PAD, PAD + NZ, 16):
         coefficients(phe, coef, inv, diag, row, 16)
 
     for k in range(2):
@@ -279,10 +270,20 @@
     near = jnp.where(outside, 0.0, turned(ne[...]))
     near_edge[main, :] = near
     pe[2, main, :] = pltpu.roll(near, 64, 1)
+    inner = [(row, 16) for row in range(PAD, PAD + NZ, 16)]
+    rims = [(PAD - 8, 16), (PAD + NZ - 8, 16)]
+    for row, rows in inner:
+        start(lame, inv, coef, near_edge, own_edge, s5, W[5], False, row, rows)
+    for m in range(5, 0, -1):
+        cotangent_sweep(ss, s_up, coef, m, inner)
     for k in range(2):
         to_x[6 + k].wait_recv()
         for j in range(2):
             rese[4 * k + j, main, :] = turned(rx_res[k, 4 * j : 4 * j + 4])
+    for row, rows in inner:
+        start(rese, inv, coef, near_edge, own_edge, e0, W[0], True, row, rows)
+    for m in range(5):
+        residual_sweep(ee, e_up, coef, m, inner)
 
     for copy in to_d:
         copy.wait_recv()
@@ -300,11 +301,10 @@
         near_edge[at : at + 8, :] = jnp.where(
             lane < 64, below, jnp.where(lane < 96, above, own_edge[at : at + 8, :])
         )
-    for r in (PAD - 8, PAD, PAD + NZ - 8, PAD + NZ):
-        coefficients(phe, coef, inv, diag, r, 8)
-
-    for row in range(PAD - 8, PAD + NZ + 8, 24):
-        starts(lame, rese, inv, coef, near_edge, own_edge, s5, e0, row, 24)
+    for row, rows in rims:
+        coefficients(phe, coef, inv, diag, row, rows)
+        start(lame, inv, coef, near_edge, own_edge, s5, W[5], False, row, rows)
+        start(rese, inv, coef, near_edge, own_edge, e0, W[0], True, row, rows)
 
     for s in range(2):
         spare = 0 if s == 0 else 7
@@ -317,22 +317,20 @@
             c_own = coef[ZD if s == 0 else ZU, c, own : own + 1, :]
             c_other = coef[ZU if s == 0 else ZD, c, other : other + 1, :]
             sign = -W[5] if s == 0 else W[5]
-            s5[c, own : own + 1, :] += sign * (c_own * speed)
-            s5[c, other : other + 1, :] -= sign * (c_other * speed)
-            e0[c, own : own + 1, :] += W[0] * (c_own * step)
-            e0[c, other : other + 1, :] -= W[0] * (c_other * step)
-    for copy in to_z + to_x + to_d:
+            ss[5, c, own : own + 1, :] += sign * (c_own * speed)
+            ss[5, c, other : other + 1, :] -= sign * (c_other * speed)
+            ee[0, c, own : own + 1, :] += W[0] * (c_own * step)
+            ee[0, c, other : other + 1, :] -= W[0] * (c_other * step)
+    for m in range(5):
+        cotangent_sweep(ss, s_up, coef, 5 - m, rims)
+        residual_sweep(ee, e_up, coef, m, rims)
+    for copy in to_z + to_x[:0] + to_x[0:] + to_d:
         copy.wait_send()
-
-
-def edge_out_p0(ps):
-    return ps.at[0:1]
 
 
 def neighbours(src, coef, tiles, have, row, rows):
     lane = lanes(rows)
     cur = {c: src[c, pl.ds(row, rows), :] for c in have}
-    out = {}
     for c in tiles:
         v = cur[c]
         near = [
@@ -344,83 +342,93 @@
             src[c, pl.ds(row - 1, rows), :],
         ]
         prod = [coef[k, c, pl.ds(row, rows), :] * near[k] for k in range(6)]
-        out[c] = (v, (prod[0] + prod[1]) + (prod[2] + prod[3]) + (prod[4] + prod[5]))
-    return out
-
-
-def chains(coef, s5, e0, pe, diag, vt, gd, gp, gf, s, e, rr, out):
-    step = 24
-
-    def sweep(src, dst, tiles, have, keep, scale, first=PAD - 8, last=PAD + NZ + 8):
-        for row in range(first, last, step):
-            for c, (v, total) in neighbours(src, coef, tiles, have, row, step).items():
-                dst[c, pl.ds(row, step), :] = keep * v + scale * total
-
-    ss = [s.at[m] for m in range(5)] + [s5]
-    ee = [e0] + [e.at[m] for m in range(5)]
-    every, middle = range(6), range(1, 5)
-    for m in range(5, 0, -1):
-        sweep(ss[m], ss[m - 1], every if m == 5 else middle, every if m >= 4 else middle,
-              W[m - 1] / W[m] * (1.0 - W[m]), W[m - 1])
-    for m in range(5):
-        tiles = (range(1, 6), middle, middle, middle, range(2, 5))[m]
-        have = (every, range(1, 6), middle, middle, middle)[m]
-        sweep(ee[m], ee[m + 1], tiles, have, W[m + 1] / W[m] * (1.0 - W[m]), W[m + 1])
-
-    for row in (PAD,):
-        for c in range(2, 5):
+        yield c, v, near, (prod[0] + prod[1]) + (prod[2] + prod[3]) + (prod[4] + prod[5])
+
+
+EVERY, MIDDLE = range(6), range(1, 5)
+
+
+def sweep(src, dst, up, coef, tiles, have, keep, scale, places):
+    for row, rows in places:
+        for c, v, near, total in neighbours(src, coef, tiles, have, row, rows):
+            dst[c, pl.ds(row, rows), :] = keep * v + scale * total
+            if c in (2, 3):
+                up[0, c - 2, pl.ds(row, rows), :] = near[XU]
+                up[1, c - 2, pl.ds(row, rows), :] = near[YU]
+
+
+def cotangent_sweep(ss, s_up, coef, m, places):
+    sweep(
+        ss.at[m], ss.at[m - 1], s_up.at[m - 1], coef, EVERY if m == 5 else MIDDLE, EVERY if m >= 4 else MIDDLE,
+        W[m - 1] / W[m] * (1.0 - W[m]), W[m - 1], places,
+    )
+
+
+def residual_sweep(ee, e_up, coef, m, places):
+    tiles = (range(1, 6), MIDDLE, MIDDLE, MIDDLE, range(2, 5))[m]
+    have = (EVERY, range(1, 6), MIDDLE, MIDDLE, MIDDLE)[m]
+    sweep(ee.at[m], ee.at[m + 1], e_up.at[m], coef, tiles, have, W[m + 1] / W[m] * (1.0 - W[m]), W[m + 1], places)
+
+
+def gradients(coef, ss, ee, s_up, e_up, pe, diag, vt, gd_hbm, gp_hbm, gf_hbm, rr, out, gd, gp, gf, sem):
+    for c in range(2, 5):
+        for row in range(PAD, PAD + NZ + 8, 8):
+            at = slice(row, row + 8)
             total = None
             for m in range(6):
-                term = ss[m][c, pl.ds(row, 136), :] * ee[m][c, pl.ds(row, 136), :] * (1.0 / W[m])
+                term = ss[m, c, at, :] * ee[m, c, at, :] * (1.0 / W[m])
                 total = term if total is None else total + term
-            rr[c - 2, pl.ds(row, 136), :] = total
-
-    for i in range(16):
-        row = PAD + 8 * i
-        own = 8 * i
-        lane = lanes(8)
-        last = (lane & 31) == 31
-
-        def rises(ref, c, at):
-            v = ref[at, pl.ds(row, 8), :]
-            after = ref[at + 1, pl.ds(row, 8), :]
-            return v, (
-                x_up(v, after, lane),
-                jnp.where(last, 0.0, y_up(v)),
-                ref[at, pl.ds(row + 1, 8), :],
-            )
-
-        for j in range(2):
-            c = 2 + j
-            p, up = rises(pe, c, j)
-            rise = [p - u for u in up]
-            grads = [None] * 3
-            total = None
-            for m in range(6):
-                v, up = rises(ss[m], c, c)
-                for a in range(3):
-                    term = (v - up[a]) * rise[a]
-                    grads[a] = term if grads[a] is None else grads[a] + term
-                total = v if total is None else total + v
-                v, up = rises(ee[m], c, c)
-                rise = [r + (v - u) for r, u in zip(rise, up)]
-            v, up = rises(rr, c, j)
-            out[0, j, pl.ds(own, 8), :] = total
+            rr[c - 2, at, :] = total
+    lane = lanes(8)
+    last = (lane & 31) == 31
+    copies = []
+
+    def give(src, dst):
+        copy = pltpu.make_async_copy(src, dst, sem.at[len(copies)])
+        copy.start()
+        copies.append(copy)
+
+    for j in range(2):
+        c = 2 + j
+        for row in range(PAD, PAD + NZ, 8):
+            at, next_at, own = slice(row, row + 8), slice(row + 1, row + 9), slice(row - PAD, row - PAD + 8)
+
+            def rises(v, x_next, y_next, z_next):
+                return v - x_next, v - jnp.where(last, 0.0, y_next), v - z_next
+
+            p = pe[j, at, :]
+            rise = rises(p, x_up(p, pe[j + 1, at, :], lane), y_up(p), pe[j, next_at, :])
+            ((_, v, near, total),) = neighbours(ss.at[0], coef, (c,), range(c - 1, c + 2), row, 8)
+            out[1, j, own, :] = diag[j, at, :] * ((1.0 / W[0] - 1.0) * v + total)
+            source = v
+            fall = rises(v, near[XU], near[YU], near[ZU])
+            grads = [f * r for f, r in zip(fall, rise)]
+            for m in range(1, 6):
+                v = ee[m - 1, c, at, :]
+                step = rises(v, e_up[m - 1, 0, j, at, :], e_up[m - 1, 1, j, at, :], ee[m - 1, c, next_at, :])
+                rise = [r + d for r, d in zip(rise, step)]
+                v = ss[m, c, at, :]
+                source = source + v
+                fall = rises(v, s_up[m - 1, 0, j, at, :], s_up[m - 1, 1, j, at, :], ss[m, c, next_at, :])
+                grads = [g + f * r for g, f, r in zip(grads, fall, rise)]
+            v = ee[5, c, at, :]
+            step = rises(v, x_up(v, ee[5, c + 1, at, :], lane), y_up(v), ee[5, c, next_at, :])
+            rise = [r + d for r, d in zip(rise, step)]
+            out[0, j, own, :] = source
+            v = rr[j, at, :]
+            up = (x_up(v, rr[j + 1, at, :], lane), jnp.where(last, 0.0, y_up(v)), rr[j, next_at, :])
             for a in range(3):
-                out[2 + a, j, pl.ds(own, 8), :] = (
-                    vt[a, j, pl.ds(own, 8), :] * rise[a] - grads[a] - (v + up[a])
-                )
-        for c, (v, total) in neighbours(ss[0], coef, (2, 3), middle, row, 8).items():
-            out[1, c - 2, pl.ds(own, 8), :] = diag[c - 2, pl.ds(row, 8), :] * (
-                (1.0 / W[0] - 1.0) * v + total
-            )
-
-    for j in range(2):
+                out[2 + a, j, own, :] = vt[a, j, own, :] * rise[a] - grads[a] - (v + up[a])
         part = slice(4 * j, 4 * j + 4)
         gd[part] = jnp.transpose(out[0, j]).reshape(4, NY, NZ)
+        give(gd.at[part], gd_hbm.at[part])
         gp[part] = jnp.transpose(out[1, j]).reshape(4, NY, NZ)
+        give(gp.at[part], gp_hbm.at[part])
         for a in range(3):
             gf[a, part] = jnp.transpose(out[2 + a, j]).reshape(4, NY, NZ)
+            give(gf.at[a, part], gf_hbm.at[a, part])
+    for copy in copies:
+        copy.wait()
 
 
 def per_device(divergence, pressure_start, phase, velocity_cot):
@@ -436,14 +444,16 @@
         exchange,
         out_shape=[
             shape((6, *tiles), F32),
-            shape(tiles, F32),
-            shape(tiles, F32),
+            shape((6, *tiles), F32),
+            shape((6, *tiles), F32),
+            shape((5, 2, 2, ROWS, 128), F32),
+            shape((5, 2, 2, ROWS, 128), F32),
             shape((3, ROWS, 128), F32),
             shape((2, ROWS, 128), F32),
             shape((3, 2, NZ, 128), F32),
         ],
         in_specs=[pl.BlockSpec(memory_space=pltpu.HBM)] * 4,
-        out_specs=[vmem] * 6,
+        out_specs=[vmem] * 8,
         scratch_shapes=[
             pltpu.VMEM(block, jnp.int32),
             pltpu.VMEM(block, F32),
@@ -480,18 +490,20 @@
     )(*args)
     return tuple(
         pl.pallas_call(
-            chains,
+            gradients,
             out_shape=[shape(block, F32), shape(block, F32), shape((3, *block), F32)],
-            in_specs=[vmem] * 6,
-            out_specs=[vmem] * 3,
+            in_specs=[vmem] * 8,
+            out_specs=[pl.BlockSpec(memory_space=pltpu.HBM)] * 3,
             scratch_shapes=[
-                pltpu.VMEM((5, *tiles), F32),
-                pltpu.VMEM((5, *tiles), F32),
                 pltpu.VMEM((3, ROWS, 128), F32),
                 pltpu.VMEM((5, 2, NZ, 128), F32),
+                pltpu.VMEM(block, F32),
+                pltpu.VMEM(block, F32),
+                pltpu.VMEM((3, *block), F32),
+                dma((10,)),
             ],
-            compiler_params=pltpu.CompilerParams(vmem_limit_bytes=24 << 20),
-            name="chains",
+            compiler_params=pltpu.CompilerParams(vmem_limit_bytes=16 << 20),
+            name="gradients",
         )(*made)
     )
 

time: 24 us -> 22.8 us (0.950)
  Pallas kernels: 23.2 us -> 22.1 us
    pallas_call x2, Pallas kernels: 23.2 us -> 22.1 us  [the longest x1 20.2 us: per_device(): pl.pallas_call(exchange, out_shape=[shape((6, *tiles), F32), shape((6, *t...]
where the time goes in v3:
time: 22.8 us; the launch traced here: 22.7 us
  Pallas kernels  22.1 us (97%)
  between operations  0.64 us (3%)
    pallas_call x1, Pallas kernels, per_device(): pl.pallas_call(exchange, out_shape=[shape((6, *tiles), F32), shape((6, *t...  20.2 us
    pallas_call x1, Pallas kernels, per_device(): pl.pallas_call(gradients, out_shape=[shape(block, F32), shape(block, F32)...  1.87 us

profile of v3, /device:TPU:32, one launch (start us, length us, event | category | flops | bytes accessed | tf_op | source)
XLA Modules:
  0.0 22.7 jit_solution(5365964338037466984)
XLA Ops:
  0.6 20.2 %exchange.1 = (f32[6,6,160,128]{3,2,1,0:T(8,128)S(1)}, f32[6,6,160,128]{3,2,1,0:T(8,128)S(1)}, f32[6,6,160,128]{3,2,1,0:T(8,128)S(1)}, f32[5,2,2,160,128]{4,3,2,...) custom-call(f32[8,32,128]{2,1,0:T(8,128)} %dv_hbm.1, ...), custom_call_target="tpu_custom_call" | custom-call | tf_op jit(solution)/shard_map/exchange/pallas_call | solution.py:443
  20.9 1.9 %gradients.1 = (f32[8,32,128]{2,1,0:T(8,128)}, f32[8,32,128]{2,1,0:T(8,128)}, f32[3,8,32,128]{3,2,1,0:T(8,128)}) custom-call(f32[6,6,160,128]{3,2,1,0:T(8,128)S(1)} %get-tuple-element.11.coef, f32[6,6,160,128]{3,2,1,0:T(8,128)S(1)} %get-tuple-element.12.ss, f32[6,6,160,128]{3,2,1,0:T(8,128)S(1)} %get-tuple-element.13.ee, ...), custom_call_target="tpu_custom_call" | custom-call | tf_op jit(solution)/shard_map/gradients/pallas_call | solution.py:492

commit v4 on v3

--- a/solution.py
+++ b/solution.py
@@ -148,8 +148,15 @@
     z_after, z_before = (w, lax.rem(n + 1, nn)), (w, lax.rem(n + nn - 1, nn))
     s5, e0 = ss.at[5], ee.at[0]
     barrier = pltpu.get_barrier_semaphore()
-    for device in (x_after, x_before, z_after, z_before):
-        pl.semaphore_signal(barrier, inc=1, device_id=device, device_id_type=MESH)
+    inside_x = (w > 0, w < nw - 1)
+    inside_z = (n > 0, n < nn - 1)
+    partners = ((inside_x[1], x_after), (inside_x[0], x_before), (inside_z[1], z_after), (inside_z[0], z_before))
+    for there, device in partners:
+
+        @pl.when(there)
+        def _():
+            pl.semaphore_signal(barrier, inc=1, device_id=device, device_id_type=MESH)
+
     loads = [
         pltpu.make_async_copy(src, dst, in_sem.at[k])
         for k, (src, dst) in enumerate(((ph_hbm, ph), (ps_hbm, ps), (dv_hbm, dv), (vc_hbm, vc)))
@@ -170,6 +177,18 @@
             phe[c, r : r + PAD, :] = jnp.zeros((PAD, 128), F32)
             ss[5, c, r : r + PAD, :] = jnp.zeros((PAD, 128), F32)
             ee[0, c, r : r + PAD, :] = jnp.zeros((PAD, 128), F32)
+    for k in range(2):
+
+        @pl.when(jnp.logical_not(inside_x[k]))
+        def _():
+            rx_lam[k] = jnp.zeros((8, NY, NZ), F32)
+            rx_res[k] = jnp.zeros((8, NY, NZ), F32)
+            rd[k] = jnp.zeros((2, 7, 8, 128), F32)
+
+        @pl.when(jnp.logical_not(inside_z[k]))
+        def _():
+            rz[k] = jnp.zeros((7, 8, 128), F32)
+
     for load in loads:
         load.wait()
 
@@ -197,16 +216,12 @@
             zs[side, 3 * j + 2] = jnp.where(spare, pe[j, line : line + 1, :], rese[2 + j, at : at + 8, :])
         zs[side, 6] = own_edge[at : at + 8, :]
 
-    pl.semaphore_wait(barrier, 4)
-
-    def send(src, dst, send_sem, recv_sem, device):
-        copy = pltpu.make_async_remote_copy(src, dst, send_sem, recv_sem, device_id=device, device_id_type=MESH)
-        copy.start()
-        return copy
-
-    to_z = [
-        send(zs.at[s], rz.at[s], send_z.at[s], recv_z.at[s], device) for s, device in ((0, z_after), (1, z_before))
-    ]
+    pl.semaphore_wait(barrier, 4 - jnp.where(w == 0, 1, 0) - jnp.where(w == nw - 1, 1, 0) - jnp.where(n == 0, 1, 0) - jnp.where(n == nn - 1, 1, 0))
+
+    def remote(src, dst, send_sem, recv_sem, device):
+        return pltpu.make_async_remote_copy(src, dst, send_sem, recv_sem, device_id=device, device_id_type=MESH)
+
+    to_z = [remote(zs.at[s], rz.at[s], send_z.at[s], recv_z.at[s], device) for s, device in ((0, z_after), (1, z_before))]
     pieces = (
         (ph_hbm.at[1:8], rx_ph.at[0, 1:8], x_after),
         (ph_hbm.at[0:7], rx_ph.at[1, 0:7], x_before),
@@ -217,18 +232,35 @@
         (res.at[3:8], rx_res.at[0, 3:8], x_after),
         (res.at[0:6], rx_res.at[1, 0:6], x_before),
     )
-    to_x = []
-    for k, (src, dst, device) in enumerate(pieces):
-        if k == 99:
-            for copy in to_x[0:0]:
-                copy.wait_send()
-        to_x.append(send(src, dst, send_x.at[k], recv_x.at[k], device))
-
-    inside_x = (w > 0, w < nw - 1)
-    inside_z = (n > 0, n < nn - 1)
-    to_d = []
+    to_x = [remote(src, dst, send_x.at[k], recv_x.at[k], device) for k, (src, dst, device) in enumerate(pieces)]
+    to_d = [
+        remote(rz.at[s], rd.at[k, s], send_d.at[k, s], recv_d.at[k, s], device)
+        for s in range(2)
+        for k, device in ((0, x_after), (1, x_before))
+    ]
+
+    def act(copies, inside, side, what):
+        @pl.when(inside[side])
+        def _():
+            for copy in copies:
+                what(copy)
+
+    def start_all(copies, inside):
+        act(copies[0::2], inside, 1, lambda copy: copy.start())
+        act(copies[1::2], inside, 0, lambda copy: copy.start())
+
+    def sent(copies, inside):
+        act(copies[0::2], inside, 1, lambda copy: copy.wait_send())
+        act(copies[1::2], inside, 0, lambda copy: copy.wait_send())
+
+    def received(copy, inside, side):
+        act([copy], inside, side, lambda copy: copy.wait_recv())
+
+    start_all(to_z, inside_z)
+    start_all(to_x, inside_x)
+
     for s in range(2):
-        to_z[s].wait_recv()
+        received(to_z[s], inside_z, s)
         at = PAD - 8 if s == 0 else PAD + NZ
         spare = row8 == (0 if s == 0 else 7)
         line = PAD if s == 0 else PAD + NZ - 1
@@ -245,11 +277,10 @@
                 pe[j, at : at + 1, :] = pressure[7:8, :]
             rz[s, 3 * j + 1] = jnp.where(spare, speed, rz[s, 3 * j + 1])
             rz[s, 3 * j + 2] = jnp.where(spare, pressure - pe[j, line : line + 1, :], rz[s, 3 * j + 2])
-        for k, device in ((0, x_after), (1, x_before)):
-            to_d.append(send(rz.at[s], rd.at[k, s], send_d.at[k, s], recv_d.at[k, s], device))
+        start_all(to_d[2 * s : 2 * s + 2], inside_x)
 
     for k in range(2):
-        to_x[k].wait_recv()
+        received(to_x[k], inside_x, k)
         for j in range(2):
             block = turned(rx_ph[k, 4 * j : 4 * j + 4].astype(F32))
             phe[4 * k + j, main, :] = jnp.where(inside_x[k], block, 2.0)
@@ -258,11 +289,11 @@
         coefficients(phe, coef, inv, diag, row, 16)
 
     for k in range(2):
-        to_x[2 + k].wait_recv()
+        received(to_x[2 + k], inside_x, k)
         for j in range(2):
             lame[4 * k + j, main, :] = turned(rx_lam[k, 4 * j : 4 * j + 4])
     for k in range(2):
-        to_x[4 + k].wait_recv()
+        received(to_x[4 + k], inside_x, k)
     lane128 = lanes(NZ)
     outside = ((lane128 < 64) & jnp.logical_not(inside_x[0])) | (
         (lane128 >= 64) & (lane128 < 96) & jnp.logical_not(inside_x[1])
@@ -277,7 +308,7 @@
     for m in range(5, 0, -1):
         cotangent_sweep(ss, s_up, coef, m, inner)
     for k in range(2):
-        to_x[6 + k].wait_recv()
+        received(to_x[6 + k], inside_x, k)
         for j in range(2):
             rese[4 * k + j, main, :] = turned(rx_res[k, 4 * j : 4 * j + 4])
     for row, rows in inner:
@@ -285,8 +316,9 @@
     for m in range(5):
         residual_sweep(ee, e_up, coef, m, inner)
 
-    for copy in to_d:
-        copy.wait_recv()
+    for k in range(2):
+        received(to_d[k], inside_x, k)
+        received(to_d[2 + k], inside_x, k)
     lane = lanes(8)
     for s in range(2):
         at = PAD - 8 if s == 0 else PAD + NZ
@@ -324,8 +356,9 @@
     for m in range(5):
         cotangent_sweep(ss, s_up, coef, 5 - m, rims)
         residual_sweep(ee, e_up, coef, m, rims)
-    for copy in to_z + to_x[:0] + to_x[0:] + to_d:
-        copy.wait_send()
+    sent(to_z, inside_z)
+    sent(to_x, inside_x)
+    sent(to_d, inside_x)
 
 
 def neighbours(src, coef, tiles, have, row, rows):

time: 22.8 us -> 20.4 us (0.89)
  the two profiles are of different devices: /device:TPU:32 before, /device:TPU:96 now
where the time goes in v4:
time: 20.4 us; the launch traced here: 20.3 us
  Pallas kernels  19.7 us (97%)
  between operations  0.64 us (3%)
    pallas_call x1, Pallas kernels, per_device(): pl.pallas_call(exchange, out_shape=[shape((6, *tiles), F32), shape((6, *t...  17.8 us
    pallas_call x1, Pallas kernels, per_device(): pl.pallas_call(gradients, out_shape=[shape(block, F32), shape(block, F32)...  1.87 us

profile of v4, /device:TPU:96, one launch (start us, length us, event | category | flops | bytes accessed | tf_op | source)
XLA Modules:
  0.0 20.3 jit_solution(8385696525333678459)
XLA Ops:
  0.6 17.8 %exchange.1 = (f32[6,6,160,128]{3,2,1,0:T(8,128)S(1)}, f32[6,6,160,128]{3,2,1,0:T(8,128)S(1)}, f32[6,6,160,128]{3,2,1,0:T(8,128)S(1)}, f32[5,2,2,160,128]{4,3,2,...) custom-call(f32[8,32,128]{2,1,0:T(8,128)} %dv_hbm.1, ...), custom_call_target="tpu_custom_call" | custom-call | tf_op jit(solution)/shard_map/exchange/pallas_call | solution.py:476
  18.4 1.9 %gradients.1 = (f32[8,32,128]{2,1,0:T(8,128)}, f32[8,32,128]{2,1,0:T(8,128)}, f32[3,8,32,128]{3,2,1,0:T(8,128)}) custom-call(f32[6,6,160,128]{3,2,1,0:T(8,128)S(1)} %get-tuple-element.11.coef, f32[6,6,160,128]{3,2,1,0:T(8,128)S(1)} %get-tuple-element.12.ss, f32[6,6,160,128]{3,2,1,0:T(8,128)S(1)} %get-tuple-element.13.ee, ...), custom_call_target="tpu_custom_call" | custom-call | tf_op jit(solution)/shard_map/gradients/pallas_call | solution.py:525
